TPU v7x, 32 devices: a whole 2x2x4 slice. The times are simulated.
32 devices in a mesh: seq: 16 (over z, y, x), head: 2 (over core).
Axes of the slice: x: 2, y: 2, z: 4, core: 2. Of those that a mesh axis runs over, the one named last changes fastest.
Arguments:
- inputs: bfloat16 [4, 2048, 768], P(None, ('seq', 'head')), may hold values from -6 to 6
- cotangent: bfloat16 [4, 2048, 768], P(None, ('seq', 'head')), may hold values from -6 to 6
- lengths: int32 [4], replicated, may hold values from 512 to 2048, as said below
- query_weight: bfloat16 [2, 768, 768], P(None, None, 'head'), may hold values from -0.375 to 0.375
- key_weight: bfloat16 [2, 768, 768], P(None, None, 'head'), may hold values from -0.375 to 0.375
- value_weight: bfloat16 [2, 768, 768], P(None, None, 'head'), may hold values from -0.21875 to 0.21875
- conv_weight: float32 [2, 12, 33], P(None, 'head'), may hold values from -0.6 to 0.6
- out_weight: bfloat16 [2, 768, 768], P(None, 'head'), may hold values from -0.3125 to 0.3125
- gain_one: float32 [2, 768], replicated, may hold values from 0.1 to 1.9
- shift_one: float32 [2, 768], replicated, may hold values from -1.5 to 1.5
- up_weight: bfloat16 [2, 768, 3072], P(None, None, 'head'), may hold values from -0.21875 to 0.21875
- up_bias: float32 [2, 3072], P(None, 'head'), may hold values from -2.5 to 2.5
- down_weight: bfloat16 [2, 3072, 768], P(None, 'head'), may hold values from -0.15625 to 0.15625
- gain_two: float32 [2, 768], replicated, may hold values from 0.1 to 1.9
- shift_two: float32 [2, 768], replicated, may hold values from -1.5 to 1.5
Outputs:
- output: float32 [4, 2048, 768], P(None, ('seq', 'head'))
- grad_inputs: float32 [4, 2048, 768], P(None, ('seq', 'head'))
- query_grad: float32 [2, 768, 768], P(None, 'seq', 'head')
- key_grad: float32 [2, 768, 768], P(None, 'seq', 'head')
- value_grad: float32 [2, 768, 768], P(None, 'seq', 'head')
- conv_grad: float32 [2, 12, 33], replicated
- out_grad: float32 [2, 768, 768], P(None, 'head', 'seq')
- gain_one_grad: float32 [2, 768], replicated
- shift_one_grad: float32 [2, 768], replicated
- up_grad: float32 [2, 768, 3072], P(None, 'seq', 'head')
- up_bias_grad: float32 [2, 3072], replicated
- down_grad: float32 [2, 3072, 768], P(None, 'head', 'seq')
- gain_two_grad: float32 [2, 768], replicated
- shift_two_grad: float32 [2, 768], replicated
Inputs may be any that keep to these rules, and one draw needn't show every extreme that they name: `lengths`: one document, drawn from the seed, has length 2048.
All inputs are finite; a program needn't handle non-finite values.
Results may differ from a plain program's by a relative error of at most 0.02.
Values may be sent and summed in bfloat16 or wider, within the bound.
No kernel may reach another device: no remote copies, remote signals or barrier semaphores. Data moves between devices by JAX's collectives and lax.ppermute only.
A program may use at most 256 MiB of HBM per device.

v0:
```python
import jax
import jax.numpy as jnp
from jax import lax
from jax.experimental import pallas as pl
from jax.experimental.pallas import tpu as pltpu
from jax.sharding import Mesh, PartitionSpec as P

HEADS = 12
HEAD_DIM = 64
LANDMARKS = 64
TAPS = 33
RIM = TAPS // 2
PINV_STEPS = 6
LAYERS = 2
OWN_HEADS = 2
OWN_COLS = OWN_HEADS * HEAD_DIM
SCALE = HEAD_DIM ** (-0.5)
EPS = 1e-05
MASKED = -1e30
FF_TILE = 512
VMEM_LIMIT = 56 * 1024 * 1024

f32 = jnp.float32
bf16 = jnp.bfloat16

NN = ((1,), (0,))
NT = ((1,), (1,))
TN = ((0,), (0,))


def dg(a, b, dims):
    return lax.dot_general(a, b, (dims, ((), ())), preferred_element_type=f32)


def split2(x):
    hi = x.astype(bf16)
    return hi, (x - hi.astype(f32)).astype(bf16)


def split3(x):
    hi = x.astype(bf16)
    rest = x - hi.astype(f32)
    mid = rest.astype(bf16)
    return hi, mid, (rest - mid.astype(f32)).astype(bf16)


def dot3(a, b, dims):
    a1, a2 = split2(a)
    b1, b2 = split2(b)
    return dg(a1, b1, dims) + (dg(a1, b2, dims) + dg(a2, b1, dims))


def mm(a, b):
    a1, a2, a3 = split3(a)
    b1, b2, b3 = split3(b)
    n = b.shape[1]
    top = jnp.concatenate([b1, b2, b3], axis=1)
    low = jnp.concatenate([b1, b2, jnp.zeros_like(b3)], axis=1)
    wide = dg(jnp.concatenate([a1, a2], axis=1), jnp.concatenate([top, low], axis=0), NN)
    last = dg(a3, b1, NN)
    return wide[:, :n] + (wide[:, n : 2 * n] + (wide[:, 2 * n :] + last))


def head_mask(rows, cols):
    r = lax.broadcasted_iota(jnp.int32, (rows, cols), 0) // HEAD_DIM
    c = lax.broadcasted_iota(jnp.int32, (rows, cols), 1) // HEAD_DIM
    return r == c


def spread(x):
    n = x.shape[1]
    tall = jnp.concatenate([x] * (n // HEAD_DIM), axis=0)
    return jnp.where(head_mask(n, n), tall, 0.0)


def collect(x):
    n = x.shape[1]
    x = jnp.where(head_mask(n, n), x, 0.0)
    total = x[0:HEAD_DIM]
    for h in range(1, n // HEAD_DIM):
        total = total + x[h * HEAD_DIM : (h + 1) * HEAD_DIM]
    return total


def head_max(s):
    lane = lax.broadcasted_iota(jnp.int32, s.shape, 1) // HEAD_DIM
    out = s
    for h in range(s.shape[1] // HEAD_DIM):
        top = jnp.max(jnp.where(lane == h, s, MASKED), axis=1, keepdims=True)
        out = jnp.where(lane == h, top, out)
    return out


def head_sum(e):
    n = e.shape[1]
    ones = jnp.where(head_mask(n, n), 1.0, 0.0).astype(bf16)
    e1, e2 = split2(e)
    return dg(e1, ones, NN) + dg(e2, ones, NN)


def down_form(lanes):
    n = lanes.shape[1]
    return collect(jnp.broadcast_to(lanes, (n, n)).T)


def block(ref, b):
    return ref[:, 256 * b : 256 * (b + 1)]


def norm_rows(r):
    mean = jnp.mean(r, axis=-1, keepdims=True)
    c = r - mean
    q = lax.rsqrt(jnp.mean(c * c, axis=-1, keepdims=True) + EPS)
    return c * q, q


def norm_pull(r, gy, gain):
    n, q = norm_rows(r)
    dgain = jnp.sum(gy * n, axis=0, keepdims=True)
    dshift = jnp.sum(gy, axis=0, keepdims=True)
    a = gy * gain
    am = jnp.mean(a, axis=-1, keepdims=True)
    anm = jnp.mean(a * n, axis=-1, keepdims=True)
    return q * (a - am - n * anm), dgain, dshift


def conv_block(padded, taps, rows):
    acc = None
    for res in range(8):
        sh = padded if res == 0 else padded[res : res + rows + 24]
        for a in range(5):
            r = 8 * a + res
            if r < TAPS:
                term = sh[8 * a : 8 * a + rows] * taps[r : r + 1]
                acc = term if acc is None else acc + term
    return acc


def padded_chunk(mid_ref, prev_ref, next_ref, c, rows, lanes):
    return jnp.concatenate(
        [
            prev_ref[RIM * c : RIM * (c + 1), lanes],
            mid_ref[rows * c : rows * (c + 1), lanes],
            next_ref[RIM * c : RIM * (c + 1), lanes],
        ],
        axis=0,
    )


def call(body, outs, args, specs=None, out_specs=None, grid=None, scratch=(), cost=None):
    kw = {}
    if grid is not None:
        kw["grid"] = grid
    if specs is not None:
        kw["in_specs"] = specs
    if out_specs is not None:
        kw["out_specs"] = out_specs
    if cost is not None:
        kw["cost_estimate"] = pl.CostEstimate(flops=cost[0], bytes_accessed=cost[1], transcendentals=0)
    return pl.pallas_call(
        body,
        out_shape=[jax.ShapeDtypeStruct(s, t) for s, t in outs],
        scratch_shapes=list(scratch),
        compiler_params=pltpu.CompilerParams(vmem_limit_bytes=VMEM_LIMIT),
        **kw,
    )(*args)


def whole(a):
    nd = len(a.shape)
    return pl.BlockSpec(a.shape, lambda *_: (0,) * nd)


def of_layer(a, layer):
    nd = len(a.shape)
    return pl.BlockSpec((1,) + a.shape[1:], lambda *_: (layer,) + (0,) * (nd - 1))


def project(xr, wq, wk, wv, valid, layer):
    rows, width = xr.shape
    half = wq[0].shape[2]

    def body(x_ref, q0, q1, k0, k1, v0, v1, valid_ref, q_ref, k_ref, v_ref):
        x = x_ref[...]
        for (w0, w1), o in (((q0, q1), q_ref), ((k0, k1), k_ref)):
            o[:, :half] = dg(x, w0[0], NN)
            o[:, half:] = dg(x, w1[0], NN)
        va = valid_ref[...]
        v_ref[:, :half] = dg(x, v0[0], NN) * va
        v_ref[:, half:] = dg(x, v1[0], NN) * va

    args = (xr, *wq, *wk, *wv, valid)
    specs = [whole(xr)] + [of_layer(w, layer) for w in (*wq, *wk, *wv)] + [whole(valid)]
    outs = [((rows, 2 * half), f32)] * 3
    return call(
        body, outs, args, specs, [whole(jax.ShapeDtypeStruct(*o)) for o in outs], (1,),
        cost=(2 * rows * width * 6 * half, 4 * width * 6 * half),
    )


def scores(q, k, v, xbar, icounts, wq, wk, valid, layer):
    rows, width = q.shape
    half = width // 2

    def body(q_ref, k_ref, v_ref, xb_ref, ic_ref, q0, q1, k0, k1, valid_ref,
             near_ref, e_ref, qm_ref, km_ref, part_ref):
        x1, x2, x3 = split3(xb_ref[...] * ic_ref[...])
        xs = jnp.concatenate([x1, x2, x3], axis=0)
        for w, o, at in ((q0, qm_ref, 0), (q1, qm_ref, half), (k0, km_ref, 0), (k1, km_ref, half)):
            p = dg(xs, w[0], NN)
            o[:, at : at + half] = (
                p[:LANDMARKS] + (p[LANDMARKS : 2 * LANDMARKS] + p[2 * LANDMARKS :])
            )
        live = valid_ref[...] > 0
        for b in range(width // 256):
            at = slice(256 * b, 256 * (b + 1))
            s = dot3(q_ref[:, at] * SCALE, spread(km_ref[:, at]), NT)
            e = jnp.exp(s - head_max(s))
            near_ref[:, at] = e / head_sum(e)
            s = dot3(k_ref[:, at], spread(qm_ref[:, at] * SCALE), NT)
            s = jnp.where(live, s, MASKED)
            top = jnp.max(s, axis=0, keepdims=True)
            e = jnp.where(live, jnp.exp(s - top), 0.0)
            e_ref[:, at] = e
            part_ref[0:LANDMARKS, at] = collect(dot3(e, v_ref[:, at], TN))
            part_ref[LANDMARKS : LANDMARKS + 8, at] = jnp.concatenate(
                [top, jnp.sum(e, axis=0, keepdims=True), jnp.zeros((6, 256), f32)], axis=0
            )

    args = (q, k, v, xbar, icounts, *wq, *wk, valid)
    specs = [whole(a) for a in (q, k, v, xbar, icounts)]
    specs += [of_layer(w, layer) for w in (*wq, *wk)] + [whole(valid)]
    outs = [((rows, width), f32)] * 2 + [((LANDMARKS, width), f32)] * 2
    outs += [((LANDMARKS + 8, width), f32)]
    return call(
        body, outs, args, specs, [whole(jax.ShapeDtypeStruct(*o)) for o in outs], (1,),
        cost=(2 * rows * width * 256 * 9, 10 * 4 * rows * width),
    )


def eye(n):
    return jnp.where(
        lax.broadcasted_iota(jnp.int32, (n, n), 0) == lax.broadcasted_iota(jnp.int32, (n, n), 1),
        1.0, 0.0,
    )


def head_total(column):
    n = column.shape[0]
    row = lax.broadcasted_iota(jnp.int32, (n, 1), 0) // HEAD_DIM
    out = column
    for h in range(n // HEAD_DIM):
        s = jnp.sum(column[h * HEAD_DIM : (h + 1) * HEAD_DIM], axis=0, keepdims=True)
        out = jnp.where(row == h, s, out)
    return out


def inverse(qm, km):
    n = qm.shape[1]

    def body(q_ref, k_ref, a_ref, z_ref, p_ref, t2_ref, t3_ref):
        ident = eye(n)
        s = mm(spread(q_ref[...] * SCALE), spread(k_ref[...]).T)
        s = jnp.where(head_mask(n, n), s, MASKED)
        e = jnp.exp(s - jnp.max(s, axis=1, keepdims=True))
        a = e / jnp.sum(e, axis=1, keepdims=True)
        a_ref[...] = a
        z = a.T / head_total(jnp.sum(a * a, axis=1, keepdims=True))
        for step in range(PINV_STEPS):
            p = mm(a, z)
            t2 = 15.0 * ident - mm(p, 7.0 * ident - p)
            t3 = 13.0 * ident - mm(p, t2)
            z_ref[step] = z
            p_ref[step] = p
            t2_ref[step] = t2
            t3_ref[step] = t3
            z = 0.25 * mm(z, t3)
        z_ref[PINV_STEPS] = z

    outs = [((n, n), f32), ((PINV_STEPS + 1, n, n), f32)] + [((PINV_STEPS, n, n), f32)] * 3
    return call(body, outs, (qm, km), cost=(2 * n**3 * 6 * 25 * 4, 4 * 26 * n * n))


def merge(parts, z):
    count, rows, n = parts.shape

    def body(p_ref, z_ref, out_ref, sum_ref):
        top = p_ref[0, LANDMARKS : LANDMARKS + 1]
        for d in range(1, count):
            top = jnp.maximum(top, p_ref[d, LANDMARKS : LANDMARKS + 1])
        total = jnp.zeros_like(top)
        carried = jnp.zeros((LANDMARKS, n), f32)
        for d in range(count):
            w = jnp.exp(p_ref[d, LANDMARKS : LANDMARKS + 1] - top)
            total = total + w * p_ref[d, LANDMARKS + 1 : LANDMARKS + 2]
            carried = carried + down_form(w) * p_ref[d, 0:LANDMARKS]
        summary = carried / down_form(total)
        sum_ref[...] = summary
        out_ref[0:LANDMARKS] = collect(mm(z_ref[PINV_STEPS], spread(summary)))
        out_ref[LANDMARKS : LANDMARKS + 8] = jnp.concatenate(
            [top, total, jnp.zeros((6, n), f32)], axis=0
        )

    return call(body, [((rows, n), f32), ((LANDMARKS, n), f32)], (parts, z))


def forward_rows(near, mixed, v, prev, nxt, taps, x, weights, gains, valid, inside, layer):
    wo, wu, wd, bias = weights
    rows, width = x.shape
    chunk = rows * RIM // prev.shape[0]
    half = width // 2
    tiles = wu[0].shape[2] // FF_TILE

    def body(near_ref, mix_ref, v_ref, prev_ref, next_ref, taps_ref, x_ref, o0, o1, u0, u1, d0, d1,
             bias_ref, g1, s1, g2, s2, valid_ref, in_ref,
             al_ref, r1_ref, fl_ref, dgelu_ref, hid_ref, r2_ref, xn_ref, xr_ref, xb_ref,
             att, first, acc):
        i = pl.program_id(0)

        @pl.when(i == 0)
        def _():
            for b in range(width // 256):
                at = slice(256 * b, 256 * (b + 1))
                att[:, at] = dot3(near_ref[:, at], spread(mix_ref[0:LANDMARKS, at]), NN)
            for b in range(width // 128):
                at = slice(128 * b, 128 * (b + 1))
                taps_here = taps_ref[:, at]
                for c in range(rows // chunk):
                    here = slice(chunk * c, chunk * (c + 1))
                    att[here, at] += conv_block(
                        padded_chunk(v_ref, prev_ref, next_ref, c, chunk, at), taps_here, chunk
                    )
            low = att[...].astype(bf16)
            al_ref[...] = low
            r1 = x_ref[...].astype(f32) + (dg(low[:, :half], o0[0], NN) + dg(low[:, half:], o1[0], NN))
            r1_ref[...] = r1
            n, _q = norm_rows(r1)
            rows1 = n * g1[layer : layer + 1] + s1[layer : layer + 1]
            first[...] = rows1
            fl_ref[...] = rows1.astype(bf16)
            acc[...] = jnp.zeros_like(acc)

        def tile(u, d):
            up = dg(fl_ref[...], u[0], NN) + bias_ref[...]
            phi = 0.5 * (1.0 + lax.erf(up * (0.5**0.5)))
            dgelu_ref[...] = phi + up * (jnp.exp(-0.5 * up * up) * 0.3989422804014327)
            hid = (up * phi).astype(bf16)
            hid_ref[...] = hid
            acc[...] += dg(hid, d[0], NN)

        @pl.when(i < tiles)
        def _():
            tile(u0, d0)

        @pl.when(i >= tiles)
        def _():
            tile(u1, d1)

        @pl.when(i == 2 * tiles - 1)
        def _():
            r2 = first[...] + acc[...]
            r2_ref[...] = r2
            n, _q = norm_rows(r2)
            xn = (n * g2[layer : layer + 1] + s2[layer : layer + 1]) * valid_ref[...]
            xn_ref[...] = xn
            xr = xn.astype(bf16)
            xr_ref[...] = xr
            xb_ref[...] = dg(in_ref[...], xr, TN)

    own = lambda i: jnp.minimum(i, tiles - 1)
    oth = lambda i: jnp.maximum(i - tiles, 0)
    up_spec = lambda f: pl.BlockSpec((1, width, FF_TILE), lambda i: (layer, 0, f(i)))
    down_spec = lambda f: pl.BlockSpec((1, FF_TILE, width), lambda i: (layer, f(i), 0))
    args = (near, mixed, v, prev, nxt, taps, x, *wo, *wu, *wd, bias, *gains, valid, inside)
    specs = [whole(a) for a in (near, mixed, v, prev, nxt, taps, x)]
    specs += [of_layer(w, layer) for w in wo]
    specs += [up_spec(own), up_spec(oth), down_spec(own), down_spec(oth)]
    specs += [pl.BlockSpec((1, FF_TILE), lambda i: (0, i))]
    specs += [whole(a) for a in (*gains, valid, inside)]
    ff = 2 * tiles * FF_TILE
    row = ((rows, width), f32)
    low = ((rows, width), bf16)
    outs = [low, row, low, ((rows, ff), f32), ((rows, ff), bf16), row, row, low,
            ((LANDMARKS, width), f32)]
    wide = pl.BlockSpec((rows, FF_TILE), lambda i: (0, i))
    out_specs = [wide if s[1] == ff else whole(jax.ShapeDtypeStruct(s, t)) for s, t in outs]
    return call(
        body, outs, args, specs, out_specs, (2 * tiles,), [pltpu.VMEM((rows, width), f32)] * 3,
        cost=(2 * rows * width * (2 * ff + width) * 2, 30 * rows * width * 4),
    )


def backward_rows(g, r1, r2, dgelu, near, mixed, q, km, weights, gains, valid, layer):
    wo, wu, wd = weights
    rows, width = r1.shape
    half = width // 2
    tiles = wu[0].shape[2] // FF_TILE

    def body(g_ref, r1_ref, r2_ref, near_ref, mix_ref, q_ref, km_ref, dgelu_ref,
             o0, o1, u0, u1, d0, d1, g1, g2, valid_ref,
             gd_ref, gu_ref, bias_ref, gr1_ref, gb_ref, gatt_ref, gqn_ref, mk_ref, small_ref, acc):
        i = pl.program_id(0)

        @pl.when(i == 0)
        def _():
            gy = g_ref[...].astype(f32) * valid_ref[...]
            gr2, dgain, dshift = norm_pull(r2_ref[...], gy, g2[layer : layer + 1])
            acc[...] = gr2
            gd_ref[...] = gr2.astype(bf16)
            small_ref[2:3] = dgain
            small_ref[3:4] = dshift

        def tile(u, d):
            gh = dg(gd_ref[...], d[0], NT)
            gu = (gh * dgelu_ref[...]).astype(bf16)
            gu_ref[...] = gu
            bias_ref[...] = jnp.sum(gu.astype(f32), axis=0, keepdims=True)
            acc[...] += dg(gu, u[0], NT)

        @pl.when(i < tiles)
        def _():
            tile(u0, d0)

        @pl.when(i >= tiles)
        def _():
            tile(u1, d1)

        @pl.when(i == 2 * tiles - 1)
        def _():
            gr1, dgain, dshift = norm_pull(r1_ref[...], acc[...], g1[layer : layer + 1])
            small_ref[0:1] = dgain
            small_ref[1:2] = dshift
            small_ref[4:8] = jnp.zeros((4, width), f32)
            gr1_ref[...] = gr1
            gb = gr1.astype(bf16)
            gb_ref[...] = gb
            gatt_ref[:, :half] = dg(gb, o0[0], NT)
            gatt_ref[:, half:] = dg(gb, o1[0], NT)
            for b in range(width // 256):
                at = slice(256 * b, 256 * (b + 1))
                gatt = gatt_ref[:, at]
                nr = near_ref[:, at]
                gn = dot3(gatt, spread(mix_ref[0:LANDMARKS, at]), NT)
                gs = nr * (gn - head_sum(nr * gn)) * SCALE
                gqn_ref[:, at] = dot3(gs, spread(km_ref[:, at]), NN)
                mk_ref[0:LANDMARKS, at] = collect(dot3(nr, gatt, TN))
                mk_ref[LANDMARKS:, at] = collect(dot3(gs, q_ref[:, at], TN))

    own = lambda i: jnp.minimum(i, tiles - 1)
    oth = lambda i: jnp.maximum(i - tiles, 0)
    up_spec = lambda f: pl.BlockSpec((1, width, FF_TILE), lambda i: (layer, 0, f(i)))
    down_spec = lambda f: pl.BlockSpec((1, FF_TILE, width), lambda i: (layer, f(i), 0))
    wide = pl.BlockSpec((rows, FF_TILE), lambda i: (0, i))
    first = (g, r1, r2, near, mixed, q, km)
    args = (*first, dgelu, *wo, *wu, *wd, *gains, valid)
    specs = [whole(a) for a in first] + [wide] + [of_layer(w, layer) for w in wo]
    specs += [up_spec(own), up_spec(oth), down_spec(own), down_spec(oth)]
    specs += [whole(a) for a in (*gains, valid)]
    ff = 2 * tiles * FF_TILE
    row = ((rows, width), f32)
    low = ((rows, width), bf16)
    outs = [low, ((rows, ff), bf16), ((1, ff), f32), row, low, row, row,
            ((2 * LANDMARKS, width), f32), ((8, width), f32)]
    out_specs = [whole(jax.ShapeDtypeStruct(s, t)) for s, t in outs]
    out_specs[1] = wide
    out_specs[2] = pl.BlockSpec((1, FF_TILE), lambda i: (0, i))
    return call(
        body, outs, args, specs, out_specs, (2 * tiles,), [pltpu.VMEM((rows, width), f32)],
        cost=(2 * rows * width * (2 * ff + width) * 2, 30 * rows * width * 4),
    )


def inverse_pull(parts, qm, km, summary, a, zs, ps, t2s, t3s):
    count, rows, n = parts.shape

    def body(g_ref, q_ref, k_ref, s_ref, a_ref, z_ref, p_ref, t2_ref, t3_ref, out_ref):
        ident = eye(n)
        mask = head_mask(n, n)
        g = g_ref[0]
        for d in range(1, count):
            g = g + g_ref[d]
        gm = spread(g[0:LANDMARKS])
        sm = s_ref[...]
        sb = spread(sm)
        a = a_ref[...]
        at = a.T
        gz = mm(gm, sb.T)
        gs = collect(mm(z_ref[PINV_STEPS].T, gm))
        ga = jnp.zeros((n, n), f32)
        for step in reversed(range(PINV_STEPS)):
            z, p, t2, t3 = z_ref[step], p_ref[step], t2_ref[step], t3_ref[step]
            zt, pt = z.T, p.T
            gt3 = 0.25 * mm(zt, gz)
            gt2 = -mm(pt, gt3)
            gt1 = -mm(pt, gt2)
            gp = -(mm(gt3, t2.T) + mm(gt2, (7.0 * ident - p).T) + gt1)
            gz = 0.25 * mm(gz, t3.T) + mm(at, gp)
            ga = ga + mm(gp, zt)
        norm = head_total(jnp.sum(a * a, axis=1, keepdims=True))
        gn = -head_total(jnp.sum(gz * at, axis=1, keepdims=True)) / (norm * norm)
        ga = ga + gz.T / norm + 2.0 * a * gn
        gsc = jnp.where(mask, a * (ga - jnp.sum(a * ga, axis=1, keepdims=True)), 0.0) * SCALE
        out_ref[0:LANDMARKS] = gs
        out_ref[LANDMARKS : 2 * LANDMARKS] = collect(mm(gsc, spread(k_ref[...])))
        out_ref[2 * LANDMARKS : 3 * LANDMARKS] = g[LANDMARKS:] + collect(
            mm(gsc.T, spread(q_ref[...]))
        )
        centre = jnp.sum(spread(gs * sm), axis=1, keepdims=True)
        out_ref[3 * LANDMARKS : 3 * LANDMARKS + 8] = jnp.broadcast_to(centre, (n, n)).T[0:8]

    return call(
        body, [((3 * LANDMARKS + 8, n), f32)], (parts, qm, km, summary, a, zs, ps, t2s, t3s),
        cost=(2 * n**3 * 6 * 52 * 4, 4 * 26 * n * n),
    )[0]


def far_pull(e, top, mixed, marks, qm, k, v, gatt, prev, nxt, vprev, vnext, taps, flipped, inside,
             icounts, valid):
    rows, width = k.shape
    chunk = rows * RIM // prev.shape[0]

    def body(e_ref, top_ref, mix_ref, mk_ref, qm_ref, k_ref, v_ref, ga_ref, prev_ref, next_ref,
             vprev_ref, vnext_ref, flip_ref, in_ref, ic_ref, valid_ref,
             gk_ref, gv_ref, gq_ref, cg_ref, gv):
        tops = mix_ref[LANDMARKS : LANDMARKS + 1]
        scale = jnp.exp(top_ref[...] - tops) / mix_ref[LANDMARKS + 1 : LANDMARKS + 2]
        ins = in_ref[...]
        ins3 = jnp.concatenate([ins, ins, ins], axis=1)
        for b in range(width // 256):
            at = slice(256 * b, 256 * (b + 1))
            far = e_ref[:, at] * scale[:, at]
            gs = spread(mk_ref[0:LANDMARKS, at])
            gf = dot3(v_ref[:, at], gs, NT)
            sc = far * (gf - mk_ref[3 * LANDMARKS : 3 * LANDMARKS + 1, at]) * SCALE
            gv[:, at] = dot3(far, gs, NN)
            gq_ref[:, at] = collect(dot3(sc, k_ref[:, at], TN))
            gkm = mk_ref[2 * LANDMARKS : 3 * LANDMARKS, at] * ic_ref[...]
            gk = dot3(sc, spread(qm_ref[:, at]), NN) + dg(
                ins3, jnp.concatenate(split3(gkm), axis=0), NN
            )
            gk_ref[:, at] = gk.astype(bf16)
        for b in range(width // 128):
            at = slice(128 * b, 128 * (b + 1))
            flip_here = flip_ref[:, at]
            sums = [None] * TAPS
            for c in range(rows // chunk):
                here = slice(chunk * c, chunk * (c + 1))
                gv[here, at] += conv_block(
                    padded_chunk(ga_ref, prev_ref, next_ref, c, chunk, at), flip_here, chunk
                )
                vp = padded_chunk(v_ref, vprev_ref, vnext_ref, c, chunk, at)
                ga = ga_ref[here, at]
                for res in range(8):
                    sh = vp if res == 0 else vp[res : res + chunk + 24]
                    for a in range(5):
                        r = 8 * a + res
                        if r < TAPS:
                            prod = ga * sh[8 * a : 8 * a + chunk]
                            s = prod[0:8]
                            for j in range(1, chunk // 8):
                                s = s + prod[8 * j : 8 * (j + 1)]
                            sums[r] = s if sums[r] is None else sums[r] + s
            for r in range(TAPS):
                cg_ref[r : r + 1, at] = jnp.sum(sums[r], axis=0, keepdims=True)
        gv_ref[...] = (gv[...] * valid_ref[...]).astype(bf16)

    args = (e, top, mixed, marks, qm, k, v, gatt, prev, nxt, vprev, vnext, flipped, inside,
            icounts, valid)
    outs = [((rows, width), bf16)] * 2 + [((LANDMARKS, width), f32), ((TAPS, width), f32)]
    return call(
        body, outs, args, scratch=[pltpu.VMEM((rows, width), f32)],
        cost=(2 * rows * width * 256 * 15, 12 * 4 * rows * width),
    )


def input_pull(gqn, gqm, marks, inside, icounts, gk, gv, gr1, wq, wk, wv, layer):
    rows, width = gqn.shape
    half = width // 2

    def body(gqn_ref, gqm_ref, mk_ref, in_ref, ic_ref, gk_ref, gv_ref, gr1_ref,
             q0, q1, k0, k1, v0, v1, gq_ref, gx_ref):
        ins = in_ref[...]
        ins3 = jnp.concatenate([ins, ins, ins], axis=1)
        gm = (gqm_ref[...] + mk_ref[LANDMARKS : 2 * LANDMARKS]) * ic_ref[...]
        gq = (gqn_ref[...] + dg(ins3, jnp.concatenate(split3(gm), axis=0), NN)).astype(bf16)
        gq_ref[...] = gq
        gx = gr1_ref[...]
        for g, w0, w1 in ((gq, q0, q1), (gk_ref[...], k0, k1), (gv_ref[...], v0, v1)):
            gx = gx + (dg(g[:, :half], w0[0], NT) + dg(g[:, half:], w1[0], NT))
        gx_ref[...] = gx

    first = (gqn, gqm, marks, inside, icounts, gk, gv, gr1)
    args = (*first, *wq, *wk, *wv)
    specs = [whole(a) for a in first] + [of_layer(w, layer) for w in (*wq, *wk, *wv)]
    outs = [((rows, width), bf16), ((rows, width), f32)]
    return call(
        body, outs, args, specs, [whole(jax.ShapeDtypeStruct(*o)) for o in outs], (1,),
        cost=(2 * rows * width * 3 * width, 8 * 4 * rows * width),
    )


def partner(x, axis, mask):
    n = lax.axis_size(axis)
    return lax.ppermute(x, axis, [(i, i ^ mask) for i in range(n)])


def swap(x):
    return partner(x, "core", 1)


def sum_over(x, axis):
    n = lax.axis_size(axis)
    if n <= 4:
        parts = [partner(x, axis, m) for m in range(1, n)]
        for p in parts:
            x = x + p
        return x
    bit = 1
    while bit < n:
        x = x + partner(x, axis, bit)
        bit *= 2
    return x


def by_core(own, oth, axis):
    first = lax.axis_index("core") == 0
    return jnp.where(
        first, jnp.concatenate([own, oth], axis=axis), jnp.concatenate([oth, own], axis=axis)
    )


def sum_doc(x):
    first = lax.axis_index("core") == 0
    half = x.shape[1] // 2
    keep = jnp.where(first, x[:, :half], x[:, half:])
    send = jnp.where(first, x[:, half:], x[:, :half])
    total = sum_over(keep + swap(send), "part")
    return by_core(total, swap(total), 1)


def sum_heads(x):
    half = x.shape[1] // 2
    total = sum_over(x[:, :half] + swap(x[:, half:]), "part")
    return jnp.concatenate([total, swap(total)], axis=1)


def owner_pieces(x):
    half = x.shape[1] // 2
    owners = half // OWN_COLS
    parts = lax.axis_size("part")
    zero = jnp.zeros((x.shape[0], OWN_COLS), x.dtype)

    def pieces(at):
        return jnp.stack(
            [x[:, at + p * OWN_COLS : at + (p + 1) * OWN_COLS] if p < owners else zero
             for p in range(parts)]
        )

    own, oth = pieces(0), pieces(half)
    first = lax.axis_index("core") == 0
    out = jnp.where(first, jnp.stack([own, oth], axis=1), jnp.stack([oth, own], axis=1))
    return out.reshape(2 * parts, x.shape[0], OWN_COLS)


def to_owners(x):
    return lax.all_to_all(owner_pieces(x), ("part", "core"), 0, 0, tiled=True)


def from_owners(x, owners):
    got = lax.all_gather(x, ("part", "core"), axis=0)
    got = got.reshape(-1, 2, *x.shape)[:owners]
    cols = [jnp.concatenate([got[p, c] for p in range(owners)], axis=1) for c in range(2)]
    return by_core(cols[0], cols[1], 1)


def own_slice(x):
    owners = x.shape[1] // 2 // OWN_COLS
    p = jnp.minimum(lax.axis_index("part"), owners - 1)
    return lax.dynamic_slice_in_dim(x, p * OWN_COLS, OWN_COLS, axis=1)


def xor_order(x, index):
    n = x.shape[0]
    bit = 1
    while bit < n:
        other = jnp.stack([x[k ^ bit] for k in range(n)])
        x = jnp.where((index & bit) > 0, other, x)
        bit *= 2
    return x


def to_docs(x):
    x = xor_order(x, lax.axis_index("doc"))
    got = [x[0]] + [partner(x[k], "doc", k) for k in range(1, x.shape[0])]
    return jnp.concatenate(got, axis=0)


def from_docs(x, docs):
    x = x.reshape(docs, -1, x.shape[-1])
    got = [x[0]] + [partner(x[k], "doc", k) for k in range(1, docs)]
    return xor_order(jnp.stack(got), lax.axis_index("doc"))


def rims(x, docs):
    rows = x.shape[0] // docs
    width = x.shape[1]
    chunks = x.reshape(docs, rows, width)
    parts = lax.axis_size("part")
    n = 2 * parts
    me = 2 * lax.axis_index("part") + lax.axis_index("core")
    doc = lax.axis_index("doc")
    axes = ("part", "core")
    prev = lax.ppermute(chunks[:, rows - RIM :], axes, [(i, (i + 1) % n) for i in range(n)])
    nxt = lax.ppermute(chunks[:, :RIM], axes, [((i + 1) % n, i) for i in range(n)])
    half = width // 2
    prev, nxt = (
        jnp.concatenate([a[..., half:], a[..., :half]], axis=-1) for a in (prev, nxt)
    )
    zero = jnp.zeros((1, RIM, width), x.dtype)
    before = xor_order(jnp.concatenate([zero, xor_order(prev, doc)[:-1]]), doc)
    after = xor_order(jnp.concatenate([xor_order(nxt, doc)[1:], zero]), doc)
    prev = jnp.where(me == 0, before, prev)
    nxt = jnp.where(me == n - 1, after, nxt)
    return prev.reshape(docs * RIM, width), nxt.reshape(docs * RIM, width)


def halve_parts(x, low_first):
    me = lax.axis_index("part")
    n = x.shape[1]
    bit = 1 if low_first else n // 2
    while n > 1:
        if low_first:
            v = x.reshape(x.shape[0], n // 2, 2, *x.shape[2:])
            axis = 2
        else:
            v = x.reshape(x.shape[0], 2, n // 2, *x.shape[2:])
            axis = 1
        mine = (me & bit) // bit
        keep = lax.dynamic_index_in_dim(v, mine, axis, keepdims=False)
        send = lax.dynamic_index_in_dim(v, 1 - mine, axis, keepdims=False)
        got = partner(send, "part", bit)
        x = (keep.astype(f32) + got.astype(f32)).astype(bf16)
        n //= 2
        bit = bit * 2 if low_first else bit // 2
    return x[:, 0]


def reduce_rows(grad):
    docs, parts = lax.axis_size("doc"), lax.axis_size("part")
    rows, cols = grad.shape
    x = grad.reshape(docs, parts, rows // (docs * parts), cols)
    cut = (cols // 256) * 128
    x = jnp.concatenate(
        [halve_parts(x[..., :cut], True), halve_parts(x[..., cut:], False)], axis=-1
    )
    x = xor_order(x, lax.axis_index("doc"))
    total = x[0].astype(f32)
    for k in range(1, docs):
        total = total + partner(x[k], "doc", k).astype(f32)
    return total


def weight_grad(left, right):
    return dg(left, right, TN).astype(bf16)


def both(x):
    return jnp.concatenate([x, swap(x)], axis=0)


def both_own(x):
    half = x.shape[1] // 2
    return jnp.concatenate([x[:, :half], swap(x[:, half:])], axis=0)


def local(inputs, cotangent, lengths, query_weight, key_weight, value_weight, conv_weight,
          out_weight, gain_one, shift_one, up_weight, up_bias, down_weight, gain_two, shift_two):
    docs, chunk, width = inputs.shape
    parts = lax.axis_size("part")
    doc, part, core = (lax.axis_index(a) for a in ("doc", "part", "core"))
    half = query_weight.shape[2]
    owners = half // OWN_COLS
    rows = docs * chunk

    length = lengths[doc]
    group = jnp.arange(docs, dtype=jnp.int32) ^ doc
    place = ((group * parts + part) * 2 + core) * chunk
    place = (place[:, None] + jnp.arange(chunk, dtype=jnp.int32)[None, :]).reshape(rows)
    valid = (place < length).astype(f32)[:, None]
    bounds = jnp.arange(LANDMARKS + 1, dtype=jnp.int32) * length // LANDMARKS
    inside = (
        (place[:, None] >= bounds[None, :-1]) & (place[:, None] < bounds[None, 1:])
    ).astype(bf16)
    icounts = 1.0 / (bounds[1:] - bounds[:-1]).astype(f32)[:, None]

    state = to_docs(inputs)
    grad = to_docs(cotangent)
    wq = (query_weight, swap(query_weight))
    wk = (key_weight, swap(key_weight))
    wv = (value_weight, swap(value_weight))
    wo = (out_weight, swap(out_weight))
    wu = (up_weight, swap(up_weight))
    wd = (down_weight, swap(down_weight))
    bias = jnp.concatenate([up_bias, swap(up_bias)], axis=1)
    conv = jnp.concatenate([conv_weight, swap(conv_weight)], axis=1)
    taps_all = jnp.repeat(jnp.swapaxes(conv, 1, 2), HEAD_DIM, axis=2)

    low = state
    xbar = dg(inside, low, TN)
    kept = []
    for layer in range(LAYERS):
        taps = taps_all[layer]
        xbar = sum_doc(xbar)
        q, k, v = project(low, wq, wk, wv, valid, layer)
        vprev, vnext = rims(v, docs)
        near, e, qm, km, part_sums = scores(q, k, v, xbar, icounts, wq, wk, valid, layer)
        top = part_sums[LANDMARKS : LANDMARKS + 1]
        qm_own, km_own = own_slice(qm), own_slice(km)
        inv = inverse(qm_own, km_own)
        merged, summary = merge(to_owners(part_sums), inv[1])
        mixed = from_owners(merged, owners)
        al, r1, fl, dgelu, hid, r2, nxt_state, nxt_low, nxt_xbar = forward_rows(
            near, mixed, v, vprev, vnext, taps, state, (wo, wu, wd, bias[layer : layer + 1]),
            (gain_one, shift_one, gain_two, shift_two), valid, inside, layer,
        )
        kept.append(dict(
            low=low, q=q, k=k, v=v, vprev=vprev, vnext=vnext, near=near, e=e, qm=qm, km=km, top=top,
            qm_own=qm_own, km_own=km_own, inv=inv, summary=summary, mixed=mixed, al=al, r1=r1,
            fl=fl, dgelu=dgelu, hid=hid, r2=r2, taps=taps,
        ))
        state, low, xbar = nxt_state, nxt_low, nxt_xbar
    output = from_docs(state, docs)

    mats = [None] * LAYERS
    smalls = [None] * LAYERS
    for layer in reversed(range(LAYERS)):
        s = kept[layer]
        gd, gu, gbias, gr1, gb, gatt, gqn, mk, small = backward_rows(
            grad, s["r1"], s["r2"], s["dgelu"], s["near"], s["mixed"], s["q"], s["km"],
            (wo, wu, wd), (gain_one, gain_two), valid, layer,
        )
        gprev, gnext = rims(gatt, docs)
        down_t = reduce_rows(weight_grad(both(gd), both_own(s["hid"])))
        up = reduce_rows(weight_grad(both(s["fl"]), both_own(gu)))
        out_t = reduce_rows(weight_grad(both(gb), both_own(s["al"])))
        a, zs, ps, t2s, t3s = s["inv"]
        pulled = inverse_pull(
            to_owners(mk), s["qm_own"], s["km_own"], s["summary"], a, zs, ps, t2s, t3s
        )
        marks = from_owners(pulled, owners)
        gk, gv, gqm, cg = far_pull(
            s["e"], s["top"], s["mixed"], marks, s["qm"], s["k"], s["v"], gatt, gprev, gnext,
            s["vprev"], s["vnext"], s["taps"], s["taps"][::-1], inside, icounts, valid,
        )
        gqm = sum_heads(gqm)
        gq, grad = input_pull(gqn, gqm, marks, inside, icounts, gk, gv, gr1, wq, wk, wv, layer)
        low2 = both(s["low"])
        qkv = reduce_rows(
            weight_grad(low2, jnp.concatenate([both_own(gq), both_own(gk), both_own(gv)], axis=1))
        )
        mats[layer] = (
            qkv[:, :half], qkv[:, half : 2 * half], qkv[:, 2 * half :], out_t.T, up, down_t.T
        )
        fh = gbias.shape[1] // 2
        gbias = by_core(gbias[:, :fh], gbias[:, fh:], 1)
        cg = jnp.sum(cg.reshape(TAPS, HEADS, HEAD_DIM), axis=-1).T
        cg = by_core(cg[: HEADS // 2], cg[HEADS // 2 :], 0)
        flat = [small[:4].reshape(-1), gbias.reshape(-1), cg.reshape(-1)]
        pad = -(HEADS * TAPS) % 128
        smalls[layer] = jnp.concatenate(flat + [jnp.zeros((pad,), f32)]).reshape(-1, 128)
    grad_inputs = from_docs(grad.astype(bf16), docs).astype(f32)

    small = jnp.stack(smalls)
    small = small + swap(small)
    small = sum_over(small, "part")
    small = sum_over(small, "doc").reshape(LAYERS, -1)
    vec = [small[:, i * width : (i + 1) * width] for i in range(4)]
    at = 4 * width
    ff = 2 * up_bias.shape[1]
    gbias = small[:, at : at + ff]
    gconv = small[:, at + ff : at + ff + HEADS * TAPS].reshape(LAYERS, HEADS, TAPS)
    m = [jnp.stack([mats[l][i] for l in range(LAYERS)]) for i in range(6)]
    return (
        output, grad_inputs, m[0], m[1], m[2], gconv, m[3], vec[0], vec[1], m[4], gbias, m[5],
        vec[2], vec[3],
    )


def solution(mesh):
    seq = ("doc", "part")
    rows = P(None, ("doc", "part", "core"), None)
    placed = (
        rows, rows, P(), P(None, None, "core"), P(None, None, "core"), P(None, None, "core"),
        P(None, "core", None), P(None, "core", None), P(), P(), P(None, None, "core"),
        P(None, "core"), P(None, "core", None), P(), P(),
    )
    outs = (
        rows, rows, P(None, seq, "core"), P(None, seq, "core"), P(None, seq, "core"), P(),
        P(None, "core", seq), P(), P(), P(None, seq, "core"), P(), P(None, "core", seq), P(), P(),
    )

    def run(*args):
        docs = args[0].shape[0]
        seq_size = mesh.shape["seq"]
        cut = Mesh(
            mesh.devices.reshape(docs, seq_size // docs, mesh.shape["head"]),
            ("doc", "part", "core"),
        )
        return jax.shard_map(local, mesh=cut, in_specs=placed, out_specs=outs, check_vma=False)(*args)

    return run
```

profile of v0, /device:TPU:0, one launch (start us, length us, event | category | flops | bytes accessed | tf_op | source)
XLA Modules:
  0.0 676.2 jit_solution(7874093668714127865)
XLA Ops:
  25.9 3.4 rev.6.flip_ref
  29.3 3.4 rev.7.flip_ref
  36.9 3.5 collective-permute-start.29
  42.6 3.8 collective-permute-start.30
  55.0 3.7 collective-permute-start.9
  66.5 4.4 shard_map.254
  70.9 6.5 shard_map.255
  83.4 4.2 all-to-all-start
  89.0 7.2 %shard_map.256 = (f32[128,128]{1,0:T(8,128)}, f32[7,128,128]{2,1,0:T(8,128)}, f32[6,128,128]{2,1,0:T(8,128)}, f32[6,128,128]{2,1,0:T(8,128)}, f32[6,128,128]{2,1,0:T(8,128)}) custom-call(f32[64,128]{1,0:T(8,128)} %get-tuple-element.613.q_ref, f32[64,128]{1,0:T(8,128)} %get-tuple-element.612.k_ref), custom_call_target="tpu_custom_call" | custom-call | flops 2516582400 | bytes 1703936 | tf_op jit(solution)/shard_map/pallas_call | solution.py:160
  100.9 10.1 %all-gather = f32[576,128]{1,0:T(8,128)S(1)} all-gather(f32[72,128]{1,0:T(8,128)} %get-tuple-element.98), channel_id=2, replica_groups=mesh['doc'=4,'part'=4,'core'=2] {'part','core'}, dimensions={0}, use_global_device_ids=true | all-gather | bytes 331776 | tf_op jit(solution)/shard_map/all_gather | solution.py:670
  113.0 17.7 %shard_map.258 = (bf16[256,768]{1,0:T(8,128)(2,1)}, f32[256,768]{1,0:T(8,128)}, bf16[256,768]{1,0:T(8,128)(2,1)}, f32[256,3072]{1,0:T(8,128)}, bf16[256,3072]{1,...) custom-call(f32[256,768]{1,0:T(8,128)} %get-tuple-element.93.near_ref, ...), custom_call_target="tpu_custom_call" | custom-call | flops 5435817984 | bytes 23592960 | tf_op jit(solution)/shard_map/pallas_call | solution.py:160
  131.1 4.5 shard_map.259
  152.8 6.4 shard_map.260
  162.3 3.4 all-to-all-start.1
  168.4 7.1 %shard_map.261 = (f32[128,128]{1,0:T(8,128)}, f32[7,128,128]{2,1,0:T(8,128)}, f32[6,128,128]{2,1,0:T(8,128)}, f32[6,128,128]{2,1,0:T(8,128)}, f32[6,128,128]{2,1,0:T(8,128)}) custom-call(f32[64,128]{1,0:T(8,128)} %constant_dynamic-slice_fusion.31.q_ref, f32[64,128]{1,0:T(8,128)} %constant_dynamic-slice_fusion.30.k_ref), custom_call_target="tpu_custom_call" | custom-call | flops 2516582400 | bytes 1703936 | tf_op jit(solution)/shard_map/pallas_call | solution.py:160
  178.5 10.1 %all-gather.1 = f32[576,128]{1,0:T(8,128)S(1)} all-gather(f32[72,128]{1,0:T(8,128)} %get-tuple-element.109), channel_id=3, replica_groups=mesh['doc'=4,'part'=4,'core'=2] {'part','core'}, dimensions={0}, use_global_device_ids=true | all-gather | bytes 331776 | tf_op jit(solution)/shard_map/all_gather | solution.py:670
  189.4 18.1 %shard_map.263 = (bf16[256,768]{1,0:T(8,128)(2,1)}, f32[256,768]{1,0:T(8,128)}, bf16[256,768]{1,0:T(8,128)(2,1)}, f32[256,3072]{1,0:T(8,128)}, bf16[256,3072]{1,...) custom-call(f32[256,768]{1,0:T(8,128)} %get-tuple-element.104.near_ref,, ...), custom_call_target="tpu_custom_call" | custom-call | flops 5435817984 | bytes 23592960 | tf_op jit(solution)/shard_map/pallas_call | solution.py:160
  207.4 16.3 %shard_map.264 = (bf16[256,768]{1,0:T(8,128)(2,1)}, bf16[256,3072]{1,0:T(8,128)(2,1)}, f32[1,3072]{1,0:T(1,128)}, f32[256,768]{1,0:T(8,128)}, bf16[256,768]{1,0:...) custom-call(bf16[256,768]{1,0:T(8,128)(2,1)} %pad_maximum_fusion.17.g_ref, ...), custom_call_target="tpu_custom_call" | custom-call | flops 5435817984 | bytes 23592960 | tf_op jit(solution)/shard_map/pallas_call | solution.py:160
  230.4 4.2 all-to-all-start.2
  245.3 5.0 collective-permute-done.26
  250.3 9.5 %collective-permute-done.27 = f32[64,768]{1,0:T(8,128)S(1)} collective-permute-done((f32[64,768]{1,0:T(8,128)S(1)}, f32[64,768]{1,0:T(8,128)S(1)}, u32[]{:S(2)}, u32[]{:S(2)}) %collective-permute-start.27) | collective-permute-done | bytes 196640 | tf_op jit(solution)/shard_map/ppermute | solution.py:604
  266.5 8.5 %shard_map.265 = f32[200,128]{1,0:T(8,128)} custom-call(f32[8,128,128]{2,1,0:T(8,128)} %all-to-all-done.2.g_ref, f32[64,128]{1,0:T(8,128)} %constant_dynamic-slice_fusion.31.q_ref, f32[64,128]{1,0:T(8,128)} %constant_dynamic-slice_fusion.30.k_ref, f32[64,128]{1,0:T(8,128)} %get-tuple-element.118.s_ref, f32[128,128]{1,0:T(8,128)} %get-tuple-element.119.a_ref, ...), custom_call_target="tpu_custom_call" | custom-call | flops 5234491392 | bytes 1703936 | tf_op jit(solution)/shard_map/pallas_call | solution.py:160
  275.0 10.3 %all-gather.2 = f32[1600,128]{1,0:T(8,128)S(1)} all-gather(f32[200,128]{1,0:T(8,128)} %shard_map.265), channel_id=4, replica_groups=mesh['doc'=4,'part'=4,'core'=2] {'part','core'}, dimensions={0}, use_global_device_ids=true | all-gather | bytes 921600 | tf_op jit(solution)/shard_map/all_gather | solution.py:670
  286.3 11.3 %shard_map.266 = (bf16[256,768]{1,0:T(8,128)(2,1)}, bf16[256,768]{1,0:T(8,128)(2,1)}, f32[64,768]{1,0:T(8,128)}, f32[33,768]{1,0:T(8,128)}) custom-call(f32[256,768]{1,0:T(8,128)} %get-tuple-element.116.e_ref, f32[1,768]{1,0:T(1,128)} %slice.1391.top_ref, f32[72,768]{1,0:T(8,128)} %broadcast_select_fusion.2.mix_ref, ...), custom_call_target="tpu_custom_call" | custom-call | flops 1509949440 | bytes 9437184 | tf_op jit(solution)/shard_map/pallas_call | solution.py:160
  320.2 3.0 collective-permute-done.94
  325.3 5.8 shard_map.267
  331.1 16.4 %shard_map.268 = (bf16[256,768]{1,0:T(8,128)(2,1)}, bf16[256,3072]{1,0:T(8,128)(2,1)}, f32[1,3072]{1,0:T(1,128)}, f32[256,768]{1,0:T(8,128)}, bf16[256,768]{1,0:...) custom-call(f32[256,768]{1,0:T(8,128)} %get-tuple-element.128.g_ref, ...), custom_call_target="tpu_custom_call" | custom-call | flops 5435817984 | bytes 23592960 | tf_op jit(solution)/shard_map/pallas_call | solution.py:160
  349.6 4.1 all-to-all-start.3
  372.0 3.0 collective-permute-done.39
  396.3 8.5 %shard_map.269 = f32[200,128]{1,0:T(8,128)} custom-call(f32[8,128,128]{2,1,0:T(8,128)} %all-to-all-done.3.g_ref, f32[64,128]{1,0:T(8,128)} %get-tuple-element.613.q_ref, f32[64,128]{1,0:T(8,128)} %get-tuple-element.612.k_ref, f32[64,128]{1,0:T(8,128)} %get-tuple-element.135.s_ref, f32[128,128]{1,0:T(8,128)} %get-tuple-element.136.a_ref, ...), custom_call_target="tpu_custom_call" | custom-call | flops 5234491392 | bytes 1703936 | tf_op jit(solution)/shard_map/pallas_call | solution.py:160
  404.8 11.4 %all-gather.3 = f32[1600,128]{1,0:T(8,128)S(1)} all-gather(f32[200,128]{1,0:T(8,128)} %shard_map.269), channel_id=5, replica_groups=mesh['doc'=4,'part'=4,'core'=2] {'part','core'}, dimensions={0}, use_global_device_ids=true | all-gather | bytes 921600 | tf_op jit(solution)/shard_map/all_gather | solution.py:670
  417.3 11.3 %shard_map.270 = (bf16[256,768]{1,0:T(8,128)(2,1)}, bf16[256,768]{1,0:T(8,128)(2,1)}, f32[64,768]{1,0:T(8,128)}, f32[33,768]{1,0:T(8,128)}) custom-call(f32[256,768]{1,0:T(8,128)} %get-tuple-element.133.e_ref, f32[1,768]{1,0:T(1,128)} %slice.1438.top_ref, f32[72,768]{1,0:T(8,128)} %broadcast_select_fusion.3.mix_ref, f32[200,768]{1,0:T(8,128)} %broadcast_select_fusion.mk_ref, ...), custom_call_target="tpu_custom_call" | custom-call | flops 1509949440 | bytes 9437184 | tf_op jit(solution)/shard_map/pallas_call | solution.py:160
  458.6 11.9 %collective-permute-done.81 = bf16[4,2,48,256]{3,2,0,1:T(8,128)(2,1)S(1)} collective-permute-done((bf16[4,2,48,256]{3,2,0,1:T(8,128)(2,1)S(1)}, bf16[4,2,48,256]{3,2,0,1:T(8,128)(2,1)S(1)}, u32[]{:S(2)}, u32[]{:S(2)}) %collective-permute-start.81) | collective-permute-done | bytes 196640 | tf_op jit(solution)/shard_map/ppermute | solution.py:604
  483.8 6.8 %collective-permute-done.124 = bf16[4,2,48,768]{3,2,0,1:T(8,128)(2,1)} collective-permute-done((bf16[4,2,48,768]{3,2,0,1:T(8,128)(2,1)}, bf16[4,2,48,768]{3,2,0,1:T(8,128)(2,1)}, u32[]{:S(2)}, u32[]{:S(2)}) %collective-permute-start.124) | collective-permute-done | bytes 589856 | tf_op jit(solution)/shard_map/ppermute | solution.py:604
  494.8 8.5 %collective-permute-done.106 = bf16[4,2,48,768]{3,2,0,1:T(8,128)(2,1)} collective-permute-done((bf16[4,2,48,768]{3,2,0,1:T(8,128)(2,1)}, bf16[4,2,48,768]{3,2,0,1:T(8,128)(2,1)}, u32[]{:S(2)}, u32[]{:S(2)}) %collective-permute-start.106) | collective-permute-done | bytes 589856 | tf_op jit(solution)/shard_map/ppermute | solution.py:604
  517.0 4.8 collective-permute-done.65
  530.4 5.6 shard_map.271
  546.6 3.2 collective-permute-done.47
  559.5 3.8 collective-permute-done.107
  566.7 5.1 collective-permute-done.66
  582.7 5.2 collective-permute-done.68
  591.8 8.1 %collective-permute-done.129 = bf16[48,1536]{1,0:T(8,128)(2,1)S(1)} collective-permute-done((bf16[48,1536]{1,0:T(8,128)(2,1)S(1)}, bf16[48,1536]{1,0:T(8,128)(2,1)S(1)}, u32[]{:S(2)}, u32[]{:S(2)}) %collective-permute-start.129) | collective-permute-done | bytes 147488 | tf_op jit(solution)/shard_map/ppermute | solution.py:604
  603.5 8.9 %collective-permute-done.111 = bf16[48,1536]{1,0:T(8,128)(2,1)S(1)} collective-permute-done((bf16[48,1536]{1,0:T(8,128)(2,1)S(1)}, bf16[48,1536]{1,0:T(8,128)(2,1)S(1)}, u32[]{:S(2)}, u32[]{:S(2)}) %collective-permute-start.111) | collective-permute-done | bytes 147488 | tf_op jit(solution)/shard_map/ppermute | solution.py:604
  614.6 6.7 collective-permute-done.116
  623.1 5.8 collective-permute-start.119
  634.5 7.2 %collective-permute-done.120 = bf16[48,1536]{1,0:T(8,128)(2,1)S(1)} collective-permute-done((bf16[48,1536]{1,0:T(8,128)(2,1)S(1)}, bf16[48,1536]{1,0:T(8,128)(2,1)S(1)}, u32[]{:S(2)}, u32[]{:S(2)}) %collective-permute-start.120) | collective-permute-done | bytes 147488 | tf_op jit(solution)/shard_map/ppermute | solution.py:604
  645.1 3.4 collective-permute-done.100
  666.0 9.1 %collective-permute-done.102 = bf16[48,1536]{1,0:T(8,128)(2,1)S(1)} collective-permute-done((bf16[48,1536]{1,0:T(8,128)(2,1)S(1)}, bf16[48,1536]{1,0:T(8,128)(2,1)S(1)}, u32[]{:S(2)}, u32[]{:S(2)}) %collective-permute-start.102) | collective-permute-done | bytes 147488 | tf_op jit(solution)/shard_map/ppermute | solution.py:604
  (835 shorter events, 322.3 us)
Async XLA Ops:
  3.8 32.3 %collective-permute-start = (bf16[64,768]{1,0:T(8,128)(2,1)}, bf16[64,768]{1,0:T(8,128)(2,1)}, u32[]{:S(2)}, u32[]{:S(2)}) collective-permute-start(bf16[64,768]{1,0:T(8,128)(2,1)} %get-tuple-element.405), channel_id=1, source_target_pairs={{0,8},{8,0},{16,24},{24,16},{1,9},{9,1},{17,25},{25,17},{2,10},{10... | collective-permute-start | bytes 294920 | tf_op jit(solution)/shard_map/ppermute | solution.py:604
  6.6 29.5 %collective-permute-start.1 = (bf16[64,768]{1,0:T(8,128)(2,1)}, bf16[64,768]{1,0:T(8,128)(2,1)}, u32[]{:S(2)}, u32[]{:S(2)}) collective-permute-start(bf16[64,768]{1,0:T(8,128)(2,1)} %get-tuple-element.404), channel_id=1, source_target_pairs={{0,16},{8,24},{16,0},{24,8},{1,17},{9,25},{17,1},{25,9},{2,18},{10... | collective-permute-start | bytes 294920 | tf_op jit(solution)/shard_map/ppermute | solution.py:604
  9.2 27.8 %collective-permute-start.2 = (bf16[64,768]{1,0:T(8,128)(2,1)}, bf16[64,768]{1,0:T(8,128)(2,1)}, u32[]{:S(2)}, u32[]{:S(2)}) collective-permute-start(bf16[64,768]{1,0:T(8,128)(2,1)} %get-tuple-element.403), channel_id=1, source_target_pairs={{0,24},{8,16},{16,8},{24,0},{1,25},{9,17},{17,9},{25,1},{2,26},{10... | collective-permute-start | bytes 294920 | tf_op jit(solution)/shard_map/ppermute | solution.py:604
  9.3 23.5 %collective-permute-start.17 = (f32[2,1536]{1,0:T(2,128)}, f32[2,1536]{1,0:T(2,128)}, u32[]{:S(2)}, u32[]{:S(2)}) collective-permute-start(f32[2,1536]{1,0:T(2,128)} %param.26), channel_id=1, source_target_pairs={{0,1},{1,0},{2,3},{3,2},{4,5},{5,4},{6,7},{7,6},{8,9},{9,8},{10,11... | collective-permute-start | bytes 36872 | tf_op jit(solution)/shard_map/ppermute | solution.py:604
  17.9 46.0 %collective-permute-start.3 = (bf16[2,768,384]{2,1,0:T(8,128)(2,1)S(1)}, bf16[2,768,384]{2,1,0:T(8,128)(2,1)S(1)}, u32[]{:S(2)}, u32[]{:S(2)}) collective-permute-start(bf16[2,768,384]{2,1,0:T(8,128)(2,1)S(1)} %copy-done), channel_id=1, source_target_pairs={{0,1},{1,0},{2,3},{3,2},{4,5},{5,4},{6,7},{7,6},{8,9},{9,8},{10,11... | collective-permute-start | bytes 3538952 | tf_op jit(solution)/shard_map/ppermute | solution.py:604
  32.8 31.4 %collective-permute-start.4 = (bf16[2,768,384]{2,1,0:T(8,128)(2,1)S(1)}, bf16[2,768,384]{2,1,0:T(8,128)(2,1)S(1)}, u32[]{:S(2)}, u32[]{:S(2)}) collective-permute-start(bf16[2,768,384]{2,1,0:T(8,128)(2,1)S(1)} %copy-done.1), channel_id=1, source_target_pairs={{0,1},{1,0},{2,3},{3,2},{4,5},{5,4},{6,7},{7,6},{8,9},{9,8},{10,11... | collective-permute-start | bytes 3538952 | tf_op jit(solution)/shard_map/ppermute | solution.py:604
  36.1 28.1 %collective-permute-start.5 = (bf16[2,768,384]{2,1,0:T(8,128)(2,1)}, bf16[2,768,384]{2,1,0:T(8,128)(2,1)S(1)}, u32[]{:S(2)}, u32[]{:S(2)}) collective-permute-start(bf16[2,768,384]{2,1,0:T(8,128)(2,1)} %v0.7), channel_id=1, source_target_pairs={{0,1},{1,0},{2,3},{3,2},{4,5},{5,4},{6,7},{7,6},{8,9},{9,8},{10,11... | collective-permute-start | bytes 3538952 | tf_op jit(solution)/shard_map/ppermute | solution.py:604
  62.7 49.2 %collective-permute-start.15 = (bf16[2,768,1536]{2,1,0:T(8,128)(2,1)}, bf16[2,768,1536]{2,1,0:T(8,128)(2,1)}, u32[]{:S(2)}, u32[]{:S(2)}) collective-permute-start(bf16[2,768,1536]{2,1,0:T(8,128)(2,1)} %u0.7), channel_id=1, source_target_pairs={{0,1},{1,0},{2,3},{3,2},{4,5},{5,4},{6,7},{7,6},{8,9},{9,8},{10,11... | collective-permute-start | bytes 14155784 | tf_op jit(solution)/shard_map/ppermute | solution.py:604
  63.6 48.3 %collective-permute-start.16 = (bf16[2,1536,768]{2,1,0:T(8,128)(2,1)}, bf16[2,1536,768]{2,1,0:T(8,128)(2,1)}, u32[]{:S(2)}, u32[]{:S(2)}) collective-permute-start(bf16[2,1536,768]{2,1,0:T(8,128)(2,1)} %d0.7), channel_id=1, source_target_pairs={{0,1},{1,0},{2,3},{3,2},{4,5},{5,4},{6,7},{7,6},{8,9},{9,8},{10,11... | collective-permute-start | bytes 14155784 | tf_op jit(solution)/shard_map/ppermute | solution.py:604
  64.0 47.9 %collective-permute-start.14 = (bf16[2,384,768]{2,1,0:T(8,128)(2,1)}, bf16[2,384,768]{2,1,0:T(8,128)(2,1)S(1)}, u32[]{:S(2)}, u32[]{:S(2)}) collective-permute-start(bf16[2,384,768]{2,1,0:T(8,128)(2,1)} %o0.7), channel_id=1, source_target_pairs={{0,1},{1,0},{2,3},{3,2},{4,5},{5,4},{6,7},{7,6},{8,9},{9,8},{10,11... | collective-permute-start | bytes 3538952 | tf_op jit(solution)/shard_map/ppermute | solution.py:604
  79.6 16.5 %collective-permute-start.12 = (f32[4,16,768]{2,1,0:T(8,128)S(1)}, f32[4,16,768]{2,1,0:T(8,128)S(1)}, u32[]{:S(2)}, u32[]{:S(2)}) collective-permute-start(f32[4,16,768]{2,1,0:T(8,128)S(1)} %get-tuple-element.274), channel_id=1, source_target_pairs={{1,0},{2,1},{3,2},{4,3},{5,4},{6,5},{7,6},{0,7},{9,8},{10,9},{11,1... | collective-permute-start | bytes 589832 | tf_op jit(solution)/shard_map/ppermute | solution.py:714
  83.4 14.6 %all-to-all-start = ((f32[8,72,128]{2,1,0:T(8,128)}), f32[8,72,128]{2,1,0:T(8,128)S(1)}, u32[]{:S(2)}, u32[]{:S(2)}) async-start(f32[8,72,128]{2,1,0:T(8,128)} %bitcast.14), calls=%async_computation | async-start | bytes 589824 | tf_op jit(solution)/shard_map/all_to_all | solution.py:666
  130.7 246.3 %collective-permute-start.59 = (bf16[256,768]{1,0:T(8,128)(2,1)}, bf16[256,768]{1,0:T(8,128)(2,1)}, u32[]{:S(2)}, u32[]{:S(2)}) collective-permute-start(bf16[256,768]{1,0:T(8,128)(2,1)} %get-tuple-element.99.x_ref), channel_id=1, source_target_pairs={{0,1},{1,0},{2,3},{3,2},{4,5},{5,4},{6,7},{7,6},{8,9},{9,8},{10,11... | collective-permute-start | bytes 1179656 | tf_op jit(solution)/shard_map/ppermute | solution.py:604
  141.1 246.6 %collective-permute-start.114 = (bf16[256,1536]{1,0:T(8,128)(2,1)}, bf16[256,1536]{1,0:T(8,128)(2,1)}, u32[]{:S(2)}, u32[]{:S(2)}) collective-permute-start(bf16[256,1536]{1,0:T(8,128)(2,1)} %get-tuple-element.245), channel_id=1, source_target_pairs={{0,1},{1,0},{2,3},{3,2},{4,5},{5,4},{6,7},{7,6},{8,9},{9,8},{10,11... | collective-permute-start | bytes 2359304 | tf_op jit(solution)/shard_map/ppermute | solution.py:604
  225.9 15.3 %collective-permute-start.32 = (f32[4,16,768]{2,1,0:T(8,128)}, f32[4,16,768]{2,1,0:T(8,128)S(1)}, u32[]{:S(2)}, u32[]{:S(2)}) collective-permute-start(f32[4,16,768]{2,1,0:T(8,128)} %get-tuple-element.264), channel_id=1, source_target_pairs={{1,0},{2,1},{3,2},{4,3},{5,4},{6,5},{7,6},{0,7},{9,8},{10,9},{11,1... | collective-permute-start | bytes 589832 | tf_op jit(solution)/shard_map/ppermute | solution.py:714
  230.4 36.1 %all-to-all-start.2 = ((f32[8,128,128]{2,1,0:T(8,128)}), f32[8,128,128]{2,1,0:T(8,128)}, u32[]{:S(2)}, u32[]{:S(2)}) async-start(f32[8,128,128]{2,1,0:T(8,128)} %bitcast.63), calls=%async_computation.2 | async-start | bytes 1048576 | tf_op jit(solution)/shard_map/all_to_all | solution.py:666
  241.2 18.7 %collective-permute-start.27 = (f32[64,768]{1,0:T(8,128)S(1)}, f32[64,768]{1,0:T(8,128)S(1)}, u32[]{:S(2)}, u32[]{:S(2)}) collective-permute-start(f32[64,768]{1,0:T(8,128)S(1)} %get-tuple-element.269), channel_id=1, source_target_pairs={{0,16},{8,24},{16,0},{24,8},{1,17},{9,25},{17,1},{25,9},{2,18},{10... | collective-permute-start | bytes 589832 | tf_op jit(solution)/shard_map/ppermute | solution.py:604
  245.3 17.1 %collective-permute-start.86 = (bf16[256,768]{1,0:T(8,128)(2,1)S(1)}, bf16[256,768]{1,0:T(8,128)(2,1)S(1)}, u32[]{:S(2)}, u32[]{:S(2)}) collective-permute-start(bf16[256,768]{1,0:T(8,128)(2,1)S(1)} %copy-done.94), channel_id=1, source_target_pairs={{0,1},{1,0},{2,3},{3,2},{4,5},{5,4},{6,7},{7,6},{8,9},{9,8},{10,11... | collective-permute-start | bytes 1179656 | tf_op jit(solution)/shard_map/ppermute | solution.py:604
  263.1 39.6 %collective-permute-start.88 = (bf16[4,2,48,128]{3,2,1,0:T(8,128)(2,1)S(1)}, bf16[4,2,48,128]{3,2,1,0:T(8,128)(2,1)S(1)}, u32[]{:S(2)}, u32[]{:S(2)}) collective-permute-start(bf16[4,2,48,128]{3,2,1,0:T(8,128)(2,1)S(1)} %dynamic-slice_bitcast_fusion.7), channel_id=1, source_target_pairs={{0,2},{2,0},{4,6},{6,4},{1,3},{3,1},{5,7},{7,5},{8,10},{10,8},{12,... | collective-permute-start | bytes 294920 | tf_op jit(solution)/shard_map/ppermute | solution.py:604
  264.9 42.1 %collective-permute-start.90 = (bf16[4,2,48,256]{3,2,0,1:T(8,128)(2,1)S(1)}, bf16[4,2,48,256]{3,2,0,1:T(8,128)(2,1)S(1)}, u32[]{:S(2)}, u32[]{:S(2)}) collective-permute-start(bf16[4,2,48,256]{3,2,0,1:T(8,128)(2,1)S(1)} %bitcast.657), channel_id=1, source_target_pairs={{0,4},{2,6},{4,0},{6,2},{1,5},{3,7},{5,1},{7,3},{8,12},{10,14},{12... | collective-permute-start | bytes 589832 | tf_op jit(solution)/shard_map/ppermute | solution.py:604
  319.6 36.6 %collective-permute-start.122 = (bf16[256,768]{1,0:T(8,128)(2,1)}, bf16[256,768]{1,0:T(8,128)(2,1)}, u32[]{:S(2)}, u32[]{:S(2)}) collective-permute-start(bf16[256,768]{1,0:T(8,128)(2,1)} %get-tuple-element.164), channel_id=1, source_target_pairs={{0,1},{1,0},{2,3},{3,2},{4,5},{5,4},{6,7},{7,6},{8,9},{9,8},{10,11... | collective-permute-start | bytes 1179656 | tf_op jit(solution)/shard_map/ppermute | solution.py:604
  320.2 37.0 %collective-permute-start.123 = (bf16[256,1536]{1,0:T(8,128)(2,1)S(1)}, bf16[256,1536]{1,0:T(8,128)(2,1)}, u32[]{:S(2)}, u32[]{:S(2)}) collective-permute-start(bf16[256,1536]{1,0:T(8,128)(2,1)S(1)} %copy-done.37), channel_id=1, source_target_pairs={{0,1},{1,0},{2,3},{3,2},{4,5},{5,4},{6,7},{7,6},{8,9},{9,8},{10,11... | collective-permute-start | bytes 2359304 | tf_op jit(solution)/shard_map/ppermute | solution.py:604
  324.5 38.2 %collective-permute-start.105 = (bf16[256,1536]{1,0:T(8,128)(2,1)}, bf16[256,1536]{1,0:T(8,128)(2,1)}, u32[]{:S(2)}, u32[]{:S(2)}) collective-permute-start(bf16[256,1536]{1,0:T(8,128)(2,1)} %get-tuple-element.251), channel_id=1, source_target_pairs={{0,1},{1,0},{2,3},{3,2},{4,5},{5,4},{6,7},{7,6},{8,9},{9,8},{10,11... | collective-permute-start | bytes 2359304 | tf_op jit(solution)/shard_map/ppermute | solution.py:604
  349.6 46.8 %all-to-all-start.3 = ((f32[8,128,128]{2,1,0:T(8,128)}), f32[8,128,128]{2,1,0:T(8,128)}, u32[]{:S(2)}, u32[]{:S(2)}) async-start(f32[8,128,128]{2,1,0:T(8,128)} %bitcast.82), calls=%async_computation.3 | async-start | bytes 1048576 | tf_op jit(solution)/shard_map/all_to_all | solution.py:666
  357.1 20.0 %collective-permute-start.61 = (bf16[256,384]{1,0:T(8,128)(2,1)}, bf16[256,384]{1,0:T(8,128)(2,1)S(1)}, u32[]{:S(2)}, u32[]{:S(2)}) collective-permute-start(bf16[256,384]{1,0:T(8,128)(2,1)} %get-tuple-element.371), channel_id=1, source_target_pairs={{0,1},{1,0},{2,3},{3,2},{4,5},{5,4},{6,7},{7,6},{8,9},{9,8},{10,11... | collective-permute-start | bytes 589832 | tf_op jit(solution)/shard_map/ppermute | solution.py:604
  362.2 15.4 %collective-permute-start.62 = (bf16[256,384]{1,0:T(8,128)(2,1)}, bf16[256,384]{1,0:T(8,128)(2,1)S(1)}, u32[]{:S(2)}, u32[]{:S(2)}) collective-permute-start(bf16[256,384]{1,0:T(8,128)(2,1)} %get-tuple-element.373), channel_id=1, source_target_pairs={{0,1},{1,0},{2,3},{3,2},{4,5},{5,4},{6,7},{7,6},{8,9},{9,8},{10,11... | collective-permute-start | bytes 589832 | tf_op jit(solution)/shard_map/ppermute | solution.py:604
  377.0 160.3 %collective-permute-start.95 = (bf16[256,768]{1,0:T(8,128)(2,1)}, bf16[256,768]{1,0:T(8,128)(2,1)}, u32[]{:S(2)}, u32[]{:S(2)}) collective-permute-start(bf16[256,768]{1,0:T(8,128)(2,1)} %get-tuple-element.158), channel_id=1, source_target_pairs={{0,1},{1,0},{2,3},{3,2},{4,5},{5,4},{6,7},{7,6},{8,9},{9,8},{10,11... | collective-permute-start | bytes 1179656 | tf_op jit(solution)/shard_map/ppermute | solution.py:604
  384.6 70.2 %collective-permute-start.63 = (bf16[4,2,48,512]{3,2,1,0:T(8,128)(2,1)}, bf16[4,2,48,512]{3,2,1,0:T(8,128)(2,1)}, u32[]{:S(2)}, u32[]{:S(2)}) collective-permute-start(bf16[4,2,48,512]{3,2,1,0:T(8,128)(2,1)} %dynamic-slice_bitcast_fusion.5), channel_id=1, source_target_pairs={{0,2},{2,0},{4,6},{6,4},{1,3},{3,1},{5,7},{7,5},{8,10},{10,8},{12,... | collective-permute-start | bytes 1179656 | tf_op jit(solution)/shard_map/ppermute | solution.py:604
  394.0 48.8 %collective-permute-start.79 = (bf16[4,2,48,128]{3,2,1,0:T(8,128)(2,1)}, bf16[4,2,48,128]{3,2,1,0:T(8,128)(2,1)}, u32[]{:S(2)}, u32[]{:S(2)}) collective-permute-start(bf16[4,2,48,128]{3,2,1,0:T(8,128)(2,1)} %dynamic-slice_bitcast_fusion.8), channel_id=1, source_target_pairs={{0,2},{2,0},{4,6},{6,4},{1,3},{3,1},{5,7},{7,5},{8,10},{10,8},{12,... | collective-permute-start | bytes 294920 | tf_op jit(solution)/shard_map/ppermute | solution.py:604
  451.6 30.1 %collective-permute-start.126 = (bf16[4,2,48,768]{3,2,0,1:T(8,128)(2,1)}, bf16[4,2,48,768]{3,2,0,1:T(8,128)(2,1)}, u32[]{:S(2)}, u32[]{:S(2)}) collective-permute-start(bf16[4,2,48,768]{3,2,0,1:T(8,128)(2,1)} %dynamic-slice_bitcast_fusion), channel_id=1, source_target_pairs={{0,4},{2,6},{4,0},{6,2},{1,5},{3,7},{5,1},{7,3},{8,12},{10,14},{12... | collective-permute-start | bytes 1769480 | tf_op jit(solution)/shard_map/ppermute | solution.py:604
  452.8 17.7 %collective-permute-start.81 = (bf16[4,2,48,256]{3,2,0,1:T(8,128)(2,1)S(1)}, bf16[4,2,48,256]{3,2,0,1:T(8,128)(2,1)S(1)}, u32[]{:S(2)}, u32[]{:S(2)}) collective-permute-start(bf16[4,2,48,256]{3,2,0,1:T(8,128)(2,1)S(1)} %bitcast.656), channel_id=1, source_target_pairs={{0,4},{2,6},{4,0},{6,2},{1,5},{3,7},{5,1},{7,3},{8,12},{10,14},{12... | collective-permute-start | bytes 589832 | tf_op jit(solution)/shard_map/ppermute | solution.py:604
  454.7 19.4 %collective-permute-start.74 = (f32[2,52,128]{2,1,0:T(8,128)S(1)}, f32[2,52,128]{2,1,0:T(8,128)S(1)}, u32[]{:S(2)}, u32[]{:S(2)}) collective-permute-start(f32[2,52,128]{2,1,0:T(8,128)S(1)} %add_add_fusion.4), channel_id=1, source_target_pairs={{0,8},{8,0},{16,24},{24,16},{1,9},{9,1},{17,25},{25,17},{2,10},{10... | collective-permute-start | bytes 159752 | tf_op jit(solution)/shard_map/ppermute | solution.py:604
  454.8 19.3 %collective-permute-start.75 = (f32[2,52,128]{2,1,0:T(8,128)S(1)}, f32[2,52,128]{2,1,0:T(8,128)S(1)}, u32[]{:S(2)}, u32[]{:S(2)}) collective-permute-start(f32[2,52,128]{2,1,0:T(8,128)S(1)} %add_add_fusion.4), channel_id=1, source_target_pairs={{0,16},{8,24},{16,0},{24,8},{1,17},{9,25},{17,1},{25,9},{2,18},{10... | collective-permute-start | bytes 159752 | tf_op jit(solution)/shard_map/ppermute | solution.py:604
  474.1 63.3 %collective-permute-start.96 = (bf16[256,1536]{1,0:T(8,128)(2,1)}, bf16[256,1536]{1,0:T(8,128)(2,1)}, u32[]{:S(2)}, u32[]{:S(2)}) collective-permute-start(bf16[256,1536]{1,0:T(8,128)(2,1)} %get-tuple-element.249), channel_id=1, source_target_pairs={{0,1},{1,0},{2,3},{3,2},{4,5},{5,4},{6,7},{7,6},{8,9},{9,8},{10,11... | collective-permute-start | bytes 2359304 | tf_op jit(solution)/shard_map/ppermute | solution.py:604
  474.1 16.5 %collective-permute-start.124 = (bf16[4,2,48,768]{3,2,0,1:T(8,128)(2,1)}, bf16[4,2,48,768]{3,2,0,1:T(8,128)(2,1)}, u32[]{:S(2)}, u32[]{:S(2)}) collective-permute-start(bf16[4,2,48,768]{3,2,0,1:T(8,128)(2,1)} %bitcast.549), channel_id=1, source_target_pairs={{0,2},{2,0},{4,6},{6,4},{1,3},{3,1},{5,7},{7,5},{8,10},{10,8},{12,... | collective-permute-start | bytes 1769480 | tf_op jit(solution)/shard_map/ppermute | solution.py:604
  476.5 26.8 %collective-permute-start.106 = (bf16[4,2,48,768]{3,2,0,1:T(8,128)(2,1)}, bf16[4,2,48,768]{3,2,0,1:T(8,128)(2,1)}, u32[]{:S(2)}, u32[]{:S(2)}) collective-permute-start(bf16[4,2,48,768]{3,2,0,1:T(8,128)(2,1)} %bitcast.551), channel_id=1, source_target_pairs={{0,2},{2,0},{4,6},{6,4},{1,3},{3,1},{5,7},{7,5},{8,10},{10,8},{12,... | collective-permute-start | bytes 1769480 | tf_op jit(solution)/shard_map/ppermute | solution.py:604
  481.7 24.7 %collective-permute-start.108 = (bf16[4,2,48,768]{3,2,0,1:T(8,128)(2,1)}, bf16[4,2,48,768]{3,2,0,1:T(8,128)(2,1)S(1)}, u32[]{:S(2)}, u32[]{:S(2)}) collective-permute-start(bf16[4,2,48,768]{3,2,0,1:T(8,128)(2,1)} %dynamic-slice_bitcast_fusion.2), channel_id=1, source_target_pairs={{0,4},{2,6},{4,0},{6,2},{1,5},{3,7},{5,1},{7,3},{8,12},{10,14},{12... | collective-permute-start | bytes 1769480 | tf_op jit(solution)/shard_map/ppermute | solution.py:604
  490.6 18.2 %collective-permute-start.41 = (f32[64,384]{1,0:T(8,128)S(1)}, f32[64,384]{1,0:T(8,128)S(1)}, u32[]{:S(2)}, u32[]{:S(2)}) collective-permute-start(f32[64,384]{1,0:T(8,128)S(1)} %copy-done.51), channel_id=1, source_target_pairs={{0,2},{2,0},{4,6},{6,4},{1,3},{3,1},{5,7},{7,5},{8,10},{10,8},{12,... | collective-permute-start | bytes 294920 | tf_op jit(solution)/shard_map/ppermute | solution.py:604
  524.3 53.3 %collective-permute-start.115 = (bf16[4,2,48,768]{3,2,0,1:T(8,128)(2,1)S(1)}, bf16[4,2,48,768]{3,2,0,1:T(8,128)(2,1)S(1)}, u32[]{:S(2)}, u32[]{:S(2)}) collective-permute-start(bf16[4,2,48,768]{3,2,0,1:T(8,128)(2,1)S(1)} %bitcast.634), channel_id=1, source_target_pairs={{0,2},{2,0},{4,6},{6,4},{1,3},{3,1},{5,7},{7,5},{8,10},{10,8},{12,... | collective-permute-start | bytes 1769480 | tf_op jit(solution)/shard_map/ppermute | solution.py:604
  525.1 53.6 %collective-permute-start.117 = (bf16[4,2,48,768]{3,2,0,1:T(8,128)(2,1)}, bf16[4,2,48,768]{3,2,0,1:T(8,128)(2,1)}, u32[]{:S(2)}, u32[]{:S(2)}) collective-permute-start(bf16[4,2,48,768]{3,2,0,1:T(8,128)(2,1)} %dynamic-slice_bitcast_fusion.1), channel_id=1, source_target_pairs={{0,4},{2,6},{4,0},{6,2},{1,5},{3,7},{5,1},{7,3},{8,12},{10,14},{12... | collective-permute-start | bytes 1769480 | tf_op jit(solution)/shard_map/ppermute | solution.py:604
  528.8 14.1 %collective-permute-start.64 = (bf16[4,1,48,512]{3,2,1,0:T(8,128)(2,1)S(1)}, bf16[4,1,48,512]{3,2,1,0:T(8,128)(2,1)}, u32[]{:S(2)}, u32[]{:S(2)}) collective-permute-start(bf16[4,1,48,512]{3,2,1,0:T(8,128)(2,1)S(1)} %copy-done.61), channel_id=1, source_target_pairs={{0,4},{2,6},{4,0},{6,2},{1,5},{3,7},{5,1},{7,3},{8,12},{10,14},{12... | collective-permute-start | bytes 589832 | tf_op jit(solution)/shard_map/ppermute | solution.py:604
  545.2 27.0 %collective-permute-start.50 = (bf16[256,384]{1,0:T(8,128)(2,1)S(1)}, bf16[256,384]{1,0:T(8,128)(2,1)S(1)}, u32[]{:S(2)}, u32[]{:S(2)}) collective-permute-start(bf16[256,384]{1,0:T(8,128)(2,1)S(1)} %copy-done.70), channel_id=1, source_target_pairs={{0,1},{1,0},{2,3},{3,2},{4,5},{5,4},{6,7},{7,6},{8,9},{9,8},{10,11... | collective-permute-start | bytes 589832 | tf_op jit(solution)/shard_map/ppermute | solution.py:604
  572.3 56.8 %collective-permute-start.97 = (bf16[4,2,48,768]{3,2,1,0:T(8,128)(2,1)S(1)}, bf16[4,2,48,768]{3,2,1,0:T(8,128)(2,1)S(1)}, u32[]{:S(2)}, u32[]{:S(2)}) collective-permute-start(bf16[4,2,48,768]{3,2,1,0:T(8,128)(2,1)S(1)} %dynamic-slice_bitcast_fusion.4), channel_id=1, source_target_pairs={{0,2},{2,0},{4,6},{6,4},{1,3},{3,1},{5,7},{7,5},{8,10},{10,8},{12,... | collective-permute-start | bytes 1769480 | tf_op jit(solution)/shard_map/ppermute | solution.py:604
  573.5 58.3 %collective-permute-start.99 = (bf16[4,2,48,768]{3,2,0,1:T(8,128)(2,1)S(1)}, bf16[4,2,48,768]{3,2,0,1:T(8,128)(2,1)S(1)}, u32[]{:S(2)}, u32[]{:S(2)}) collective-permute-start(bf16[4,2,48,768]{3,2,0,1:T(8,128)(2,1)S(1)} %dynamic-slice_bitcast_fusion.3), channel_id=1, source_target_pairs={{0,4},{2,6},{4,0},{6,2},{1,5},{3,7},{5,1},{7,3},{8,12},{10,14},{12... | collective-permute-start | bytes 1769480 | tf_op jit(solution)/shard_map/ppermute | solution.py:604
  602.3 26.6 %collective-permute-start.52 = (bf16[4,2,48,512]{3,2,1,0:T(8,128)(2,1)S(1)}, bf16[4,2,48,512]{3,2,1,0:T(8,128)(2,1)S(1)}, u32[]{:S(2)}, u32[]{:S(2)}) collective-permute-start(bf16[4,2,48,512]{3,2,1,0:T(8,128)(2,1)S(1)} %dynamic-slice_bitcast_fusion.6), channel_id=1, source_target_pairs={{0,2},{2,0},{4,6},{6,4},{1,3},{3,1},{5,7},{7,5},{8,10},{10,8},{12,... | collective-permute-start | bytes 1179656 | tf_op jit(solution)/shard_map/ppermute | solution.py:604
  621.3 22.5 %collective-permute-start.54 = (bf16[4,2,48,640]{3,2,0,1:T(8,128)(2,1)S(1)}, bf16[4,2,48,640]{3,2,0,1:T(8,128)(2,1)S(1)}, u32[]{:S(2)}, u32[]{:S(2)}) collective-permute-start(bf16[4,2,48,640]{3,2,0,1:T(8,128)(2,1)S(1)} %bitcast.636), channel_id=1, source_target_pairs={{0,4},{2,6},{4,0},{6,2},{1,5},{3,7},{5,1},{7,3},{8,12},{10,14},{12... | collective-permute-start | bytes 1474568 | tf_op jit(solution)/shard_map/ppermute | solution.py:604
  656.5 18.5 %collective-permute-start.102 = (bf16[48,1536]{1,0:T(8,128)(2,1)S(1)}, bf16[48,1536]{1,0:T(8,128)(2,1)S(1)}, u32[]{:S(2)}, u32[]{:S(2)}) collective-permute-start(bf16[48,1536]{1,0:T(8,128)(2,1)S(1)} %get-tuple-element.320), channel_id=1, source_target_pairs={{0,16},{8,24},{16,0},{24,8},{1,17},{9,25},{17,1},{25,9},{2,18},{10... | collective-permute-start | bytes 442376 | tf_op jit(solution)/shard_map/ppermute | solution.py:604
  659.0 16.0 %collective-permute-start.103 = (bf16[48,1536]{1,0:T(8,128)(2,1)S(1)}, bf16[48,1536]{1,0:T(8,128)(2,1)S(1)}, u32[]{:S(2)}, u32[]{:S(2)}) collective-permute-start(bf16[48,1536]{1,0:T(8,128)(2,1)S(1)} %get-tuple-element.319), channel_id=1, source_target_pairs={{0,24},{8,16},{16,8},{24,0},{1,25},{9,17},{17,9},{25,1},{2,26},{10... | collective-permute-start | bytes 442376 | tf_op jit(solution)/shard_map/ppermute | solution.py:604
  (185 other events, 1372.2 us)
where the time goes:
time: 687 us; the launch traced here: 676 us
  Pallas kernels  160 us (23%)
  waiting for transfers between devices  154 us (22%)
  starting transfers between devices  152 us (22%)
  local copies, waits for them, and re-layouts  102 us (15%)
  other arithmetic  45.9 us (7%)
  blocking collectives  41.9 us (6%)
  matrix products  16.4 us (2%)
    pallas_call x18, Pallas kernels, call(): pl.pallas_call(body, out_shape=[jax.ShapeDtypeStruct(s, t) for s, t in ou...  160 us
    ppermute x123, waiting for transfers between devices, partner(): return lax.ppermute(x, axis, [(i, i ^ mask) for i in range(n)])  151 us
    ppermute x123, starting transfers between devices, partner(): return lax.ppermute(x, axis, [(i, i ^ mask) for i in range(n)])  125 us
    all_gather x4, blocking collectives, from_owners(): got = lax.all_gather(x, ('part', 'core'), axis=0)  41.9 us
    dot_general x9, matrix products, dg(): return lax.dot_general(a, b, (dims, ((), ())), preferred_element_type=f32)  16.4 us
    all_to_all x4, starting transfers between devices, to_owners(): return lax.all_to_all(owner_pieces(x), ('part', 'core'), 0, 0, tiled=True)  15.9 us
    unnamed x219, local copies, waits for them, and re-layouts  14.7 us
  transfers between devices with their start and end apart: 135, of which 49 were waited for; matrix products, arithmetic and copies ran while one was open for 22% of the time, Pallas kernels for 21%

commit v1 on v0

v1 whole, which is shorter than its diff:
```python
import jax
import jax.numpy as jnp
from jax import lax
from jax.experimental import pallas as pl
from jax.experimental.pallas import tpu as pltpu
from jax.sharding import Mesh, PartitionSpec as P

HEADS = 12
HEAD_DIM = 64
LANDMARKS = 64
TAPS = 33
RIM = TAPS // 2
PINV_STEPS = 6
LAYERS = 2
OWN_HEADS = 2
OWN_COLS = OWN_HEADS * HEAD_DIM
SCALE = HEAD_DIM ** (-0.5)
EPS = 1e-05
MASKED = -1e30
FF_TILE = 512
VMEM_LIMIT = 52 * 1024 * 1024

f32 = jnp.float32
bf16 = jnp.bfloat16

NN = ((1,), (0,))
NT = ((1,), (1,))
TN = ((0,), (0,))


def dg(a, b, dims):
    return lax.dot_general(a, b, (dims, ((), ())), preferred_element_type=f32)


def split2(x):
    hi = x.astype(bf16)
    return hi, (x - hi.astype(f32)).astype(bf16)


def split3(x):
    hi = x.astype(bf16)
    rest = x - hi.astype(f32)
    mid = rest.astype(bf16)
    return hi, mid, (rest - mid.astype(f32)).astype(bf16)


def dot3(a, b, dims):
    a1, a2 = split2(a)
    b1, b2 = split2(b)
    return dg(a1, b1, dims) + (dg(a1, b2, dims) + dg(a2, b1, dims))


def mm(a, b):
    a1, a2, a3 = split3(a)
    b1, b2, b3 = split3(b)
    n = b.shape[1]
    top = jnp.concatenate([b1, b2, b3], axis=1)
    low = jnp.concatenate([b1, b2, jnp.zeros_like(b3)], axis=1)
    wide = dg(jnp.concatenate([a1, a2], axis=1), jnp.concatenate([top, low], axis=0), NN)
    last = dg(a3, b1, NN)
    return wide[:, :n] + (wide[:, n : 2 * n] + (wide[:, 2 * n :] + last))


def head_mask(rows, cols):
    r = lax.broadcasted_iota(jnp.int32, (rows, cols), 0) // HEAD_DIM
    c = lax.broadcasted_iota(jnp.int32, (rows, cols), 1) // HEAD_DIM
    return r == c


def spread(x):
    n = x.shape[1]
    tall = jnp.concatenate([x] * (n // HEAD_DIM), axis=0)
    return jnp.where(head_mask(n, n), tall, 0.0)


def collect(x):
    n = x.shape[1]
    x = jnp.where(head_mask(n, n), x, 0.0)
    total = x[0:HEAD_DIM]
    for h in range(1, n // HEAD_DIM):
        total = total + x[h * HEAD_DIM : (h + 1) * HEAD_DIM]
    return total


def head_max(s):
    lane = lax.broadcasted_iota(jnp.int32, s.shape, 1) // HEAD_DIM
    out = s
    for h in range(s.shape[1] // HEAD_DIM):
        top = jnp.max(jnp.where(lane == h, s, MASKED), axis=1, keepdims=True)
        out = jnp.where(lane == h, top, out)
    return out


def head_sum(e):
    n = e.shape[1]
    ones = jnp.where(head_mask(n, n), 1.0, 0.0).astype(bf16)
    e1, e2 = split2(e)
    return dg(e1, ones, NN) + dg(e2, ones, NN)


def down_form(lanes):
    n = lanes.shape[1]
    return collect(jnp.broadcast_to(lanes, (n, n)).T)


def norm_rows(r):
    mean = jnp.mean(r, axis=-1, keepdims=True)
    c = r - mean
    q = lax.rsqrt(jnp.mean(c * c, axis=-1, keepdims=True) + EPS)
    return c * q, q


def norm_pull(r, gy, gain):
    n, q = norm_rows(r)
    dgain = jnp.sum(gy * n, axis=0, keepdims=True)
    dshift = jnp.sum(gy, axis=0, keepdims=True)
    a = gy * gain
    am = jnp.mean(a, axis=-1, keepdims=True)
    anm = jnp.mean(a * n, axis=-1, keepdims=True)
    return q * (a - am - n * anm), dgain, dshift


def conv_block(padded, taps, rows, flip=False):
    acc = None
    for res in range(8):
        sh = padded if res == 0 else padded[res : res + rows + 24]
        for a in range(5):
            r = 8 * a + res
            if r < TAPS:
                t = TAPS - 1 - r if flip else r
                term = sh[8 * a : 8 * a + rows] * taps[t : t + 1]
                acc = term if acc is None else acc + term
    return acc


def place():
    return lax.axis_index("part"), lax.axis_index("core")


def padded_chunk(mid_ref, prev_ref, next_ref, c, rows, lanes, chunks):
    part, core = place()
    parts = lax.axis_size("part")
    first = jnp.where(jnp.logical_and(part == 0, core == 0), 1, 0)
    last = jnp.where(jnp.logical_and(part == parts - 1, core == 1), 1, 0)
    zero_before = jnp.logical_and(first == 1, c == 0)
    zero_after = jnp.logical_and(last == 1, c == chunks - 1)
    at_prev = RIM * jnp.maximum(c - first, 0)
    at_next = RIM * jnp.minimum(c + last, chunks - 1)
    before = prev_ref[pl.ds(pl.multiple_of(at_prev, RIM), RIM), lanes]
    after = next_ref[pl.ds(pl.multiple_of(at_next, RIM), RIM), lanes]
    return jnp.concatenate(
        [
            jnp.where(zero_before, 0.0, before),
            mid_ref[rows * c : rows * (c + 1), lanes],
            jnp.where(zero_after, 0.0, after),
        ],
        axis=0,
    )


def write_rims(x, tail_ref, head_ref, chunks):
    rows = x.shape[0] // chunks
    half = x.shape[1] // 2
    for c in range(chunks):
        here = slice(RIM * c, RIM * (c + 1))
        for ref, at in ((tail_ref, rows * (c + 1) - RIM), (head_ref, rows * c)):
            ref[here, :half] = x[at : at + RIM, half:]
            ref[here, half:] = x[at : at + RIM, :half]


def write_pieces(out_ref, rows, own, oth):
    _, core = place()
    parts = out_ref.shape[0] // 2
    for p in range(parts):
        out_ref[2 * p + core, rows] = own(p)
        out_ref[2 * p + 1 - core, rows] = oth(p)


def read_owned(got_ref, rows, owners):
    _, core = place()
    return jnp.concatenate(
        [got_ref[2 * p + core, rows] for p in range(owners)]
        + [got_ref[2 * p + 1 - core, rows] for p in range(owners)],
        axis=1,
    )


def own_lanes(owners):
    at = jnp.minimum(place()[0], owners - 1) * OWN_COLS
    return pl.ds(pl.multiple_of(at, OWN_COLS), OWN_COLS)


ANY = pl.BlockSpec(memory_space=pl.ANY)


class In:
    def __init__(self, buf, src=None, sem=None):
        self.buf, self.shape, self.dtype = buf, buf.shape, buf.dtype
        self.copy = None
        if src is not None:
            self.copy = pltpu.make_async_copy(src, buf, sem)
            self.copy.start()

    def wait(self):
        if self.copy is not None:
            self.copy.wait()
            self.copy = None

    def __getitem__(self, at):
        self.wait()
        return self.buf[at]


class Out:
    def __init__(self, buf, dst, next_sem, flushed):
        self.dst, self.buf, self.shape, self.dtype = dst, buf, buf.shape, buf.dtype
        self.next_sem, self.flushed, self.done = next_sem, flushed, dst is None

    def __getitem__(self, at):
        return self.buf[at]

    def __setitem__(self, at, value):
        self.buf[at] = value

    def flush(self, at=None):
        if self.dst is None:
            return
        src, dst = (self.buf, self.dst) if at is None else (self.buf.at[at], self.dst.at[at])
        copy = pltpu.make_async_copy(src, dst, self.next_sem())
        copy.start()
        self.flushed.append(copy)
        self.done = True


def call(body, ins, outs, scratch=(), cost=(0, 0), after=()):
    n, extra = len(ins), len(after)
    late = [x for x in ins if isinstance(x, tuple)]
    shapes = [x[0] if x[1] is None else jax.eval_shape(lambda v, at=x[1]: v[at], x[0]) for x in late]
    kinds = [("hbm",) if len(o) == 2 else ("vmem", "hbm") if o[2] else ("vmem",) for o in outs]
    flat = [(o[0], o[1], k) for o, ks in zip(outs, kinds) for k in ks]
    alone = [o for o in outs if len(o) == 2]

    def kernel(*refs):
        given_refs = refs[:n]
        made_refs = list(refs[n + extra : n + extra + len(flat)])
        rest = refs[n + extra + len(flat) :]
        bufs = list(rest[: len(shapes) + len(alone)])
        user, sems = rest[len(shapes) + len(alone) : -1], rest[-1]
        count = [0]

        def next_sem():
            count[0] += 1
            return sems.at[count[0] - 1]

        given, made, flushed = [], [], []
        for ref, x in zip(given_refs, ins):
            if isinstance(x, tuple):
                src = ref if x[1] is None else ref.at[x[1]]
                given.append(In(bufs.pop(0), src, next_sem()))
            else:
                given.append(In(ref))
        for ks in kinds:
            buf = made_refs.pop(0) if "vmem" in ks else bufs.pop(0)
            dst = made_refs.pop(0) if "hbm" in ks else None
            made.append(Out(buf, dst, next_sem, flushed))
        body(given, made, *user)
        for x in given:
            x.wait()
        for o in made:
            if not o.done:
                o.flush()
        for copy in flushed:
            copy.wait()

    space = {"vmem": pl.BlockSpec(memory_space=pltpu.VMEM), "hbm": pl.BlockSpec(memory_space=pltpu.HBM)}
    scratch_shapes = [pltpu.VMEM(x.shape, x.dtype) for x in shapes]
    scratch_shapes += [pltpu.VMEM(o[0], o[1]) for o in alone] + list(scratch)
    scratch_shapes += [pltpu.SemaphoreType.DMA((len(shapes) + 4 * len(outs) + 24,))]
    got = list(pl.pallas_call(
        kernel,
        out_shape=[jax.ShapeDtypeStruct(shape, t) for shape, t, _ in flat],
        in_specs=[space["hbm" if isinstance(x, tuple) else "vmem"] for x in ins] + [ANY] * extra,
        out_specs=[space[k] for _s, _t, k in flat],
        scratch_shapes=scratch_shapes,
        compiler_params=pltpu.CompilerParams(vmem_limit_bytes=VMEM_LIMIT),
        cost_estimate=pl.CostEstimate(flops=cost[0], bytes_accessed=cost[1], transcendentals=0),
    )(*[x[0] if isinstance(x, tuple) else x for x in ins], *after))
    return [tuple(got.pop(0) for _ in ks) if len(ks) == 2 else got.pop(0) for ks in kinds]


def far_off(*arrays):
    return [(x, None) for x in arrays]


class Cols:
    def __init__(self, ref, start, size):
        self.ref, self.start, self.size = ref, start, size
        self.shape = (ref.shape[0], size)

    def _at(self, at):
        if at is Ellipsis:
            return slice(None), slice(self.start, self.start + self.size)
        rows, cols = at
        first, last = cols.start or 0, self.size if cols.stop is None else cols.stop
        return rows, slice(self.start + first, self.start + last)

    def __getitem__(self, at):
        return self.ref[self._at(at)]

    def __setitem__(self, at, value):
        self.ref[self._at(at)] = value


def lanes_of(x, at, size):
    return x, (slice(None), slice(at, at + size))


def prepare_taps(conv):
    layers, _, taps = conv.shape
    width = HEADS * HEAD_DIM

    def body(ins, outs):
        (c_ref,), (t_ref,) = ins, outs
        at = lax.broadcasted_iota(jnp.int32, (16, width), 1) // HEAD_DIM
        hot = jnp.where(lax.broadcasted_iota(jnp.int32, (16, width), 0) == at, 1.0, 0.0).astype(bf16)
        for layer in range(layers):
            c1, c2, c3 = split3(c_ref[layer])
            t_ref[layer] = dg(c1, hot, TN) + (dg(c2, hot, TN) + dg(c3, hot, TN))

    return call(body, [conv], [((layers, taps, width), f32, None)])[0]


def project(xr, weights, valid, layer, chunks, after=()):
    rows, width = xr.shape
    half = width // 2

    def body(ins, outs):
        x_ref, valid_ref, w0, w1 = ins
        out, tail_ref, head_ref = outs
        x = x_ref[...]
        va = valid_ref[...]
        for i in range(3):
            cols = slice(i * half, (i + 1) * half)
            for w, at in ((w0, 2 * i * half), (w1, (2 * i + 1) * half)):
                p = dg(x, w[:, cols], NN)
                out[:, at : at + half] = p * va if i == 2 else p
        out.flush()
        write_rims(Cols(out, 2 * width, width), tail_ref, head_ref, chunks)

    outs = [((rows, 3 * width), f32)] + [((RIM * chunks, width), f32, None)] * 2
    return call(
        body, [xr, valid] + [(w, layer) for w in weights], outs, after=after,
        cost=(2 * rows * width * 6 * half, 4 * width * 6 * half),
    )


def scores(qkv, xtot, xoth, icounts, weights, valid, layer, parts):
    rows, width = qkv.shape[0], qkv.shape[1] // 3
    half = width // 2
    owners = half // OWN_COLS
    pieces = 2 * parts

    def body(ins, outs, part):
        xt_ref, xo_ref, ic_ref, w0, w1, valid_ref, kv_ref, q_ref = ins
        ne_ref, marks_ref, qk_ref, out_ref = outs
        k_ref, v_ref = (Cols(kv_ref, i * width, width) for i in range(2))
        near_ref, e_ref = (Cols(ne_ref, i * width, width) for i in range(2))
        qm_ref, km_ref = (Cols(marks_ref, i * width, width) for i in range(2))
        _, core = place()
        mark = slice(0, LANDMARKS)
        xt, xo = xt_ref[...], xo_ref[...]
        xb = jnp.concatenate(
            [jnp.where(core == 0, xt, xo), jnp.where(core == 0, xo, xt)], axis=1
        )
        x1, x2, x3 = split3(xb * ic_ref[...])
        xs = jnp.concatenate([x1, x2, x3], axis=0)
        for w, at in ((w0, 0), (w1, half)):
            p = dg(xs, w[...], NN)
            p = p[:LANDMARKS] + (p[LANDMARKS : 2 * LANDMARKS] + p[2 * LANDMARKS :])
            qm_ref[mark, at : at + half] = p[:, :half]
            km_ref[mark, at : at + half] = p[:, half:]
        own = pl.multiple_of(jnp.minimum(place()[0], owners - 1) * OWN_COLS, OWN_COLS)
        qk_ref[mark] = marks_ref[mark, pl.ds(own, OWN_COLS)]
        qk_ref[LANDMARKS : 2 * LANDMARKS] = marks_ref[mark, pl.ds(width + own, OWN_COLS)]
        live = valid_ref[...] > 0
        for b in range(width // 256):
            at = slice(256 * b, 256 * (b + 1))
            s = dot3(k_ref[:, at], spread(qm_ref[mark, at] * SCALE), NT)
            s = jnp.where(live, s, MASKED)
            top = jnp.max(s, axis=0, keepdims=True)
            e = jnp.where(live, jnp.exp(s - top), 0.0)
            e_ref[:, at] = e
            part[mark, at] = collect(dot3(e, v_ref[:, at], TN))
            last = jnp.concatenate(
                [top, jnp.sum(e, axis=0, keepdims=True), jnp.zeros((6, 256), f32)], axis=0
            )
            part[LANDMARKS : LANDMARKS + 8, at] = last
            qm_ref[LANDMARKS : LANDMARKS + 8, at] = last
            km_ref[LANDMARKS : LANDMARKS + 8, at] = jnp.zeros((8, 256), f32)
        marks_ref.flush()

        def cols(base):
            def piece(p):
                if p >= owners:
                    return jnp.zeros((LANDMARKS + 8, OWN_COLS), f32)
                return part[:, base + p * OWN_COLS : base + (p + 1) * OWN_COLS]
            return piece

        write_pieces(out_ref, slice(None), cols(0), cols(half))
        for b in range(width // 256):
            at = slice(256 * b, 256 * (b + 1))
            s = dot3(q_ref[:, at] * SCALE, spread(km_ref[mark, at]), NT)
            e = jnp.exp(s - head_max(s))
            near_ref[:, at] = e / head_sum(e)
        ne_ref.flush()

    ins = [xtot, xoth, icounts]
    ins += [(w, (layer, slice(None), slice(0, width))) for w in weights]
    ins += [valid, lanes_of(qkv, width, 2 * width), lanes_of(qkv, 0, width)]
    outs = [((rows, 2 * width), f32), ((LANDMARKS + 8, 2 * width), f32)]
    outs += [((2 * LANDMARKS, OWN_COLS), f32, None), ((pieces, LANDMARKS + 8, OWN_COLS), f32, None)]
    return call(
        body, ins, outs, [pltpu.VMEM((LANDMARKS + 8, width), f32)],
        cost=(2 * rows * width * 256 * 9, 10 * 4 * rows * width),
    )


def eye(n):
    return jnp.where(
        lax.broadcasted_iota(jnp.int32, (n, n), 0) == lax.broadcasted_iota(jnp.int32, (n, n), 1),
        1.0, 0.0,
    )


def head_total(column):
    n = column.shape[0]
    row = lax.broadcasted_iota(jnp.int32, (n, 1), 0) // HEAD_DIM
    out = column
    for h in range(n // HEAD_DIM):
        s = jnp.sum(column[h * HEAD_DIM : (h + 1) * HEAD_DIM], axis=0, keepdims=True)
        out = jnp.where(row == h, s, out)
    return out


def inverse(qk):
    n = OWN_COLS

    def body(ins, outs):
        (qk_ref,) = ins
        kept_ref, end_ref = outs
        ident = eye(n)
        s = mm(spread(qk_ref[:LANDMARKS] * SCALE), spread(qk_ref[LANDMARKS:]).T)
        s = jnp.where(head_mask(n, n), s, MASKED)
        e = jnp.exp(s - jnp.max(s, axis=1, keepdims=True))
        a = e / jnp.sum(e, axis=1, keepdims=True)
        kept_ref[0] = a
        kept_ref[1] = qk_ref[...]
        z = a.T / head_total(jnp.sum(a * a, axis=1, keepdims=True))
        for step in range(PINV_STEPS):
            p = mm(a, z)
            t2 = 15.0 * ident - mm(p, 7.0 * ident - p)
            t3 = 13.0 * ident - mm(p, t2)
            for i, m in enumerate((z, p, t2, t3)):
                kept_ref[3 + 4 * step + i] = m
            z = 0.25 * mm(z, t3)
        kept_ref[2] = z
        end_ref[...] = z

    outs = [((3 + 4 * PINV_STEPS, n, n), f32), ((n, n), f32, None)]
    return call(body, [qk], outs, cost=(2 * n**3 * 6 * 25 * 4, 4 * 26 * n * n))


def merge(parts, z):
    count, rows, n = parts.shape

    def body(ins, outs):
        (p_ref, z_ref), (out_ref, sum_ref) = ins, outs
        top = p_ref[0, LANDMARKS : LANDMARKS + 1]
        for d in range(1, count):
            top = jnp.maximum(top, p_ref[d, LANDMARKS : LANDMARKS + 1])
        total = jnp.zeros_like(top)
        carried = jnp.zeros((LANDMARKS, n), f32)
        for d in range(count):
            w = jnp.exp(p_ref[d, LANDMARKS : LANDMARKS + 1] - top)
            total = total + w * p_ref[d, LANDMARKS + 1 : LANDMARKS + 2]
            carried = carried + down_form(w) * p_ref[d, 0:LANDMARKS]
        summary = carried / down_form(total)
        sum_ref[...] = summary
        mixed = collect(mm(z_ref[...], spread(summary)))
        last = jnp.concatenate([top, total, jnp.zeros((6, n), f32)], axis=0)
        for d in range(count):
            out_ref[d, 0:LANDMARKS] = mixed
            out_ref[d, LANDMARKS : LANDMARKS + 8] = last

    return call(body, [parts, z], [((count, rows, n), f32, None), ((LANDMARKS, n), f32, None)])


def halves(x):
    half = x.shape[1] // 2
    first = place()[1] == 0
    left, right = x[:, :half], x[:, half:]
    return jnp.where(first, left, right), jnp.where(first, right, left)


def forward_rows(ne, got, qkv, prev, nxt, taps, x, weights, gains, valid, inside, layer, after=()):
    wo, wu, wd, bias = weights
    rows, width = x.shape
    chunks = prev.shape[0] // RIM
    chunk = rows // chunks
    half = width // 2
    owners = half // OWN_COLS
    ffh = wu[0].shape[2]
    tiles = ffh // FF_TILE

    def body(ins, outs, att):
        (v_ref, prev_ref, next_ref, taps_ref, got_ref, near_ref, x_ref, g1, s1, bias_ref, g2, s2,
         valid_ref, in_ref, o0, o1, u0, d0, u1, d1) = ins
        mix_ref, pack_ref, own_ref, rr_ref, dgelu_ref, xn_ref, xr_ref, keep_ref, send_ref = outs
        for b in range(width // 128):
            at = slice(128 * b, 128 * (b + 1))
            taps_here = taps_ref[layer, :, at]
            for c in range(chunks):
                padded = padded_chunk(v_ref, prev_ref, next_ref, c, chunk, at, chunks)
                att[chunk * c : chunk * (c + 1), at] = conv_block(padded, taps_here, chunk)
        mix_ref[...] = read_owned(got_ref, slice(None), owners)
        mix_ref.flush()
        for b in range(width // 256):
            at = slice(256 * b, 256 * (b + 1))
            att[:, at] += dot3(near_ref[:, at], spread(mix_ref[0:LANDMARKS, at]), NN)
        low = att[...].astype(bf16)
        own_ref[:, :half] = low[:, :half]
        pack_ref[:, width : width + half] = low[:, half:]
        r1 = x_ref[...].astype(f32) + (
            dg(low[:, :half], o0[...], NN) + dg(low[:, half:], o1[...], NN)
        )
        rr_ref[:, :width] = r1
        n, _q = norm_rows(r1)
        first = n * g1[layer : layer + 1] + s1[layer : layer + 1]
        pack_ref[:, :width] = first.astype(bf16)
        att[...] = first
        for t in range(2 * tiles):
            at = slice(t * FF_TILE, (t + 1) * FF_TILE)
            here = slice(t % tiles * FF_TILE, (t % tiles + 1) * FF_TILE)
            u, d = ((u0, d0), (u1, d1))[t // tiles]
            up = dg(pack_ref[:, :width], u[:, here], NN) + bias_ref[:, at]
            phi = 0.5 * (1.0 + lax.erf(up * (0.5**0.5)))
            dgelu_ref[:, at] = (
                phi + up * (jnp.exp(-0.5 * up * up) * 0.3989422804014327)
            ).astype(dgelu_ref.dtype)
            hid = (up * phi).astype(bf16)
            if t < tiles:
                own_ref[:, half + here.start : half + here.stop] = hid
            else:
                base = width + half
                pack_ref[:, base + here.start : base + here.stop] = hid
            att[...] += dg(hid, d[here], NN)
            if t == tiles - 1:
                own_ref.flush()
        dgelu_ref.flush()
        r2 = att[...]
        rr_ref[:, width:] = r2
        rr_ref.flush()
        n, _q = norm_rows(r2)
        xn = (n * g2[layer : layer + 1] + s2[layer : layer + 1]) * valid_ref[...]
        xn_ref[...] = xn
        xr = xn.astype(bf16)
        xr_ref[...] = xr
        pack_ref[:, width + half + ffh :] = xr
        pack_ref.flush()
        keep_ref[...], send_ref[...] = halves(dg(in_ref[...], xr, TN))

    g1, s1, g2, s2 = gains
    at = lambda w: (w, layer)
    ins = [lanes_of(qkv, 2 * width, width), prev, nxt, taps, got, lanes_of(ne, 0, width), x, g1, s1, bias, g2, s2, valid, inside,
           at(wo[0]), at(wo[1]), at(wu[0]), at(wd[0]), at(wu[1]), at(wd[1])]
    outs = [((LANDMARKS + 8, width), f32), ((rows, 2 * width + half + ffh), bf16),
            ((rows, half + ffh), bf16), ((rows, 2 * width), f32), ((rows, 2 * ffh), bf16),
            ((rows, width), f32, None), ((rows, width), bf16, None),
            ((LANDMARKS, half), f32, None), ((LANDMARKS, half), f32, None)]
    return call(
        body, ins, outs, [pltpu.VMEM((rows, width), f32)],
        cost=(2 * rows * width * (4 * ffh + width) * 2, 30 * rows * width * 4), after=after,
    )


def backward_rows(g, rr, dgelu, ne, mixed, qkv, marks, weights, gains, valid, layer, chunks, parts,
                  after=()):
    wo, wu, wd = weights
    rows, width = rr.shape[0], rr.shape[1] // 2
    half = width // 2
    owners = half // OWN_COLS
    ffh = wu[0].shape[2]
    tiles = ffh // FF_TILE
    pieces = 2 * parts

    def body(ins, outs, acc, mk):
        (g_ref, g2, valid_ref, g1, rr_ref, dgelu_ref, d0, u0, d1, u1, o0, o1, near_ref, mix_ref,
         km_ref, q_ref) = ins
        (pack_ref, gu_ref, bias_ref, gr1_ref, gatt_ref, gqn_ref, out_ref, small_ref,
         tail_ref, head_ref) = outs
        mark = slice(0, LANDMARKS)
        gy = g_ref[...].astype(f32) * valid_ref[...]
        gr2, dgain, dshift = norm_pull(rr_ref[:, width:], gy, g2[layer : layer + 1])
        acc[...] = gr2
        pack_ref[:, :width] = gr2.astype(bf16)
        small_ref[2:3] = dgain
        small_ref[3:4] = dshift
        for t in range(2 * tiles):
            at = slice(t * FF_TILE, (t + 1) * FF_TILE)
            here = slice(t % tiles * FF_TILE, (t % tiles + 1) * FF_TILE)
            u, d = ((u0, d0), (u1, d1))[t // tiles]
            gh = dg(pack_ref[:, :width], d[here], NT)
            gu = (gh * dgelu_ref[:, at].astype(f32)).astype(bf16)
            bias_ref[:, at] = jnp.sum(gu.astype(f32), axis=0, keepdims=True)
            if t < tiles:
                gu_ref[:, here] = gu
            else:
                pack_ref[:, 2 * width + here.start : 2 * width + here.stop] = gu
            acc[...] += dg(gu, u[:, here], NT)
            if t == tiles - 1:
                gu_ref.flush()
        gr1, dgain, dshift = norm_pull(rr_ref[:, :width], acc[...], g1[layer : layer + 1])
        small_ref[0:1] = dgain
        small_ref[1:2] = dshift
        small_ref[4:8] = jnp.zeros((4, width), f32)
        gr1_ref[...] = gr1
        gb = gr1.astype(bf16)
        pack_ref[:, width : 2 * width] = gb
        pack_ref.flush()
        gatt_ref[:, :half] = dg(gb, o0[...], NT)
        gatt_ref[:, half:] = dg(gb, o1[...], NT)
        write_rims(gatt_ref, tail_ref, head_ref, chunks)
        for b in range(width // 256):
            at = slice(256 * b, 256 * (b + 1))
            gatt = gatt_ref[:, at]
            nr = near_ref[:, at]
            gn = dot3(gatt, spread(mix_ref[mark, at]), NT)
            gs = nr * (gn - head_sum(nr * gn)) * SCALE
            gqn_ref[:, at] = dot3(gs, spread(km_ref[mark, at]), NN)
            mk[mark, at] = collect(dot3(nr, gatt, TN))
            mk[LANDMARKS:, at] = collect(dot3(gs, q_ref[:, at], TN))

        def cols(base):
            def piece(p):
                if p >= owners:
                    return jnp.zeros((2 * LANDMARKS, OWN_COLS), f32)
                return mk[:, base + p * OWN_COLS : base + (p + 1) * OWN_COLS]
            return piece

        write_pieces(out_ref, slice(None), cols(0), cols(half))

    g1, g2 = gains
    at = lambda w: (w, layer)
    ins = [g, g2, valid, g1, *far_off(rr, dgelu), at(wd[0]), at(wu[0]), at(wd[1]), at(wu[1]),
           at(wo[0]), at(wo[1]), lanes_of(ne, 0, width), (mixed, None), lanes_of(marks, width, width),
           lanes_of(qkv, 0, width)]
    row = ((rows, width), f32, None)
    rim = ((RIM * chunks, width), f32, None)
    outs = [((rows, 2 * width + ffh), bf16), ((rows, ffh), bf16), ((1, 2 * ffh), f32, None),
            row, row, row, ((pieces, 2 * LANDMARKS, OWN_COLS), f32, None), ((8, width), f32, None),
            rim, rim]
    return call(
        body, ins, outs,
        [pltpu.VMEM((rows, width), f32), pltpu.VMEM((2 * LANDMARKS, width), f32)],
        cost=(2 * rows * width * (4 * ffh + width) * 2, 30 * rows * width * 4), after=after,
    )


def inverse_pull(parts, summary, kept, after=()):
    count, rows, n = parts.shape

    def body(ins, outs):
        s_ref, g_ref, kept_ref = ins
        (out_ref,) = outs
        ident = eye(n)
        mask = head_mask(n, n)
        g = g_ref[0]
        for d in range(1, count):
            g = g + g_ref[d]
        gm = spread(g[0:LANDMARKS])
        sm = s_ref[...]
        sb = spread(sm)
        a = kept_ref[0]
        at = a.T
        gz = mm(gm, sb.T)
        gs = collect(mm(kept_ref[2].T, gm))
        ga = jnp.zeros((n, n), f32)
        for step in reversed(range(PINV_STEPS)):
            z, p, t2, t3 = (kept_ref[3 + 4 * step + i] for i in range(4))
            zt, pt = z.T, p.T
            gt3 = 0.25 * mm(zt, gz)
            gt2 = -mm(pt, gt3)
            gt1 = -mm(pt, gt2)
            gp = -(mm(gt3, t2.T) + mm(gt2, (7.0 * ident - p).T) + gt1)
            gz = 0.25 * mm(gz, t3.T) + mm(at, gp)
            ga = ga + mm(gp, zt)
        norm = head_total(jnp.sum(a * a, axis=1, keepdims=True))
        gn = -head_total(jnp.sum(gz * at, axis=1, keepdims=True)) / (norm * norm)
        ga = ga + gz.T / norm + 2.0 * a * gn
        gsc = jnp.where(mask, a * (ga - jnp.sum(a * ga, axis=1, keepdims=True)), 0.0) * SCALE
        centre = jnp.sum(spread(gs * sm), axis=1, keepdims=True)
        out = jnp.concatenate(
            [
                gs,
                collect(mm(gsc, spread(kept_ref[1, LANDMARKS:]))),
                g[LANDMARKS:] + collect(mm(gsc.T, spread(kept_ref[1, :LANDMARKS]))),
                jnp.broadcast_to(centre, (n, n)).T[0:8],
            ],
            axis=0,
        )
        for d in range(count):
            out_ref[d] = out

    return call(
        body, [summary, parts, (kept, None)],
        [((count, 3 * LANDMARKS + 8, n), f32, None)],
        cost=(2 * n**3 * 6 * 52 * 4, 4 * 26 * n * n), after=after,
    )[0]


def conv_pull(qkv, gatt, prev, nxt, vprev, vnext, taps, layer, after=()):
    rows, width = gatt.shape
    chunks = prev.shape[0] // RIM
    chunk = rows // chunks

    def body(ins, outs):
        v_ref, vprev_ref, vnext_ref, ga_ref, taps_ref, prev_ref, next_ref = ins
        gv_ref, cg_ref = outs
        for b in range(width // 128):
            at = slice(128 * b, 128 * (b + 1))
            taps_here = taps_ref[layer, :, at]
            sums = [None] * TAPS
            for c in range(chunks):
                here = slice(chunk * c, chunk * (c + 1))
                gv_ref[here, at] = conv_block(
                    padded_chunk(ga_ref, prev_ref, next_ref, c, chunk, at, chunks),
                    taps_here, chunk, flip=True,
                )
                vp = padded_chunk(v_ref, vprev_ref, vnext_ref, c, chunk, at, chunks)
                ga = ga_ref[here, at]
                for res in range(8):
                    sh = vp if res == 0 else vp[res : res + chunk + 24]
                    for a in range(5):
                        r = 8 * a + res
                        if r < TAPS:
                            prod = ga * sh[8 * a : 8 * a + chunk]
                            s = prod[0:8]
                            for j in range(1, chunk // 8):
                                s = s + prod[8 * j : 8 * (j + 1)]
                            sums[r] = s if sums[r] is None else sums[r] + s
            for r in range(TAPS):
                cg_ref[r : r + 1, at] = jnp.sum(sums[r], axis=0, keepdims=True)
        cg_ref[TAPS:] = jnp.zeros((40 - TAPS, width), f32)

    return call(
        body, [lanes_of(qkv, 2 * width, width), vprev, vnext, gatt, taps, prev, nxt],
        [((rows, width), f32, None), ((40, width), f32, None)],
        cost=(2 * rows * width * TAPS * 40, 4 * 4 * rows * width), after=after,
    )


def far_pull(ne, marks, mixed, got, qkv, gvc, inside, icounts, valid, after=()):
    rows, width = gvc.shape
    half = width // 2
    owners = half // OWN_COLS

    def body(ins, outs, mk, gq):
        got_ref, mix_ref, in_ref, ic_ref, e_ref, kv_ref, qm_ref, gvc_ref, valid_ref = ins
        gk_ref, gv_ref, gmid_ref, own_ref, oth_ref = outs
        k_ref, v_ref = (Cols(kv_ref, i * width, width) for i in range(2))
        mark = slice(0, LANDMARKS)
        mk[...] = read_owned(got_ref, slice(None), owners)
        gmid_ref[...] = mk[LANDMARKS : 2 * LANDMARKS]
        tops = mix_ref[LANDMARKS : LANDMARKS + 1, :]
        scale = jnp.exp(qm_ref[LANDMARKS : LANDMARKS + 1, :] - tops)
        scale = scale / mix_ref[LANDMARKS + 1 : LANDMARKS + 2, :]
        ins3 = jnp.concatenate([in_ref[...]] * 3, axis=1)
        live = valid_ref[...]
        for b in range(width // 256):
            at = slice(256 * b, 256 * (b + 1))
            far = e_ref[:, at] * scale[:, at]
            gs = spread(mk[mark, at])
            gf = dot3(v_ref[:, at], gs, NT)
            sc = far * (gf - mk[3 * LANDMARKS : 3 * LANDMARKS + 1, at]) * SCALE
            gq[:, at] = collect(dot3(sc, k_ref[:, at], TN))
            gv = dot3(far, gs, NN) + gvc_ref[:, at]
            gv_ref[:, at] = (gv * live).astype(bf16)
            gkm = mk[2 * LANDMARKS : 3 * LANDMARKS, at] * ic_ref[...]
            gk = dot3(sc, spread(qm_ref[mark, at]), NN) + dg(
                ins3, jnp.concatenate(split3(gkm), axis=0), NN
            )
            gk_ref[:, at] = gk.astype(bf16)
        own_ref[...] = gq[:, :half]
        oth_ref[...] = gq[:, half:]

    ins = [got, (mixed, None), inside, icounts, lanes_of(ne, width, width),
           lanes_of(qkv, width, 2 * width), lanes_of(marks, 0, width), gvc, valid]
    outs = [((rows, width), bf16, None)] * 2 + [((LANDMARKS, width), f32, None)]
    outs += [((LANDMARKS, half), f32, None)] * 2
    return call(
        body, ins, outs,
        [pltpu.VMEM((3 * LANDMARKS + 8, width), f32), pltpu.VMEM((LANDMARKS, width), f32)],
        cost=(2 * rows * width * 256 * 15, 12 * 4 * rows * width), after=after,
    )


def input_pull(gqn, gtot, goth, gmid, inside, icounts, gk, gv, gr1, weights, layer, low_out,
               after=()):
    rows, width = gqn.shape
    half = width // 2

    def body(ins, outs):
        (gr1_ref, gk_ref, gv_ref, w0, w1, gqn_ref, gt_ref, go_ref, gmid_ref, in_ref, ic_ref) = ins
        own_ref, oth_ref, gx_ref = outs
        gm = jnp.concatenate([gt_ref[...], go_ref[...]], axis=1)
        gm = (gm + gmid_ref[...]) * ic_ref[...]
        ins3 = jnp.concatenate([in_ref[...]] * 3, axis=1)
        gq = (gqn_ref[...] + dg(ins3, jnp.concatenate(split3(gm), axis=0), NN)).astype(bf16)
        for i, g in enumerate((gq, gk_ref[...], gv_ref[...])):
            own_ref[:, i * half : (i + 1) * half] = g[:, :half]
            oth_ref[:, i * half : (i + 1) * half] = g[:, half:]
        gx = gr1_ref[...] + (dg(own_ref[...], w0[...], NT) + dg(oth_ref[...], w1[...], NT))
        gx_ref[...] = gx.astype(gx_ref.dtype)

    ins = [gr1, gk, gv, (weights[0], layer), (weights[1], layer), gqn, gtot, goth, gmid, inside,
           icounts]
    outs = [((rows, 3 * half), bf16, None)] * 2 + [((rows, width), low_out, None)]
    return call(
        body, ins, outs, cost=(2 * rows * width * 3 * width, 8 * 4 * rows * width), after=after,
    )


def split_rows(tmp, keep_ref, send_ref, cols, me, low_first, docs, parts, r):
    bit = 1 if low_first else parts // 2
    mine = (me // bit) % 2
    for d in range(docs):
        for m in range(parts // 2):
            to = slice((d * parts // 2 + m) * r, (d * parts // 2 + m + 1) * r)
            for ref, b in ((keep_ref, mine), (send_ref, 1 - mine)):
                block_at = d * parts + (2 * m + b if low_first else m + bit * b)
                ref[to, cols] = tmp[pl.ds(pl.multiple_of(block_at * r, r), r)]


def weight_grads(arrays, lefts, rights, tiles, docs, parts, after=()):
    cols = 384
    shapes = [
        x if not isinstance(x, tuple) or x[1] is None else jax.eval_shape(lambda v, at=x[1]: v[at], x[0])
        for x in arrays
    ]
    shapes = [x[0] if isinstance(x, tuple) else x for x in shapes]
    rows, width = shapes[0].shape[0], lefts[0][2]
    r = width // (docs * parts)
    split = r % 16 == 0
    sizes = [sum(1 for t in tiles if t[3] == dest) * cols for dest in (0, 1)]

    def body(given, outs, lt, tmp):
        me = place()[0]
        done = [0, 0]
        last = None
        for left, right, t, dest in tiles:
            if left != last:
                for side in range(2):
                    i, at = lefts[left][side]
                    lt[:, side * rows : (side + 1) * rows] = given[i][:, at : at + width].T
                last = left
            both = []
            for i, at in rights[right]:
                both.append(given[i][:, at + t * cols : at + (t + 1) * cols])
            x = dg(lt[...], jnp.concatenate(both, axis=0), NN).astype(bf16)
            to = slice(done[dest] * cols, (done[dest] + 1) * cols)
            done[dest] += 1
            mine = outs[2 * dest : 2 * dest + 2] if split else outs[dest : dest + 1]
            if split:
                tmp[...] = x
                split_rows(tmp, *mine, to, me, dest == 0, docs, parts, r)
            else:
                mine[0][:, to] = x
            if to.stop == sizes[dest]:
                for o in reversed(mine):
                    o.flush()

    outs = []
    for size in sizes:
        outs += [((width // 2, size), bf16)] * 2 if split else [((width, size), bf16)]
    return call(
        body, arrays, outs, [pltpu.VMEM((width, 2 * rows), bf16), pltpu.VMEM((width, cols), bf16)],
        cost=(2 * width * 2 * rows * cols * len(tiles), 2 * width * cols * len(tiles)), after=after,
    )


def fold(sums, docs, parts, after=()):
    ka, _, kb, _ = sums
    rows = ka.shape[0] // 2
    r = rows // docs

    def body(ins, outs, ta, tb):
        me = place()[0]
        for i, (tmp, mine) in enumerate(((ta, me // 2), (tb, me % 2))):
            keep, got = ins[2 * i : 2 * i + 2]
            keep_ref, send_ref = outs[2 * i : 2 * i + 2]
            tmp[...] = (keep[...].astype(f32) + got[...].astype(f32)).astype(bf16)
            for d in range(docs):
                to = slice(d * r, (d + 1) * r)
                for ref, m in ((send_ref, 1 - mine), (keep_ref, mine)):
                    ref[to] = tmp[pl.ds(pl.multiple_of((2 * d + m) * r, r), r)]
            send_ref.flush()
            keep_ref.flush()

    outs = [((rows, x.shape[1]), bf16) for x in (ka, ka, kb, kb)]
    scratch = [pltpu.VMEM(x.shape, bf16) for x in (ka, kb)]
    return call(body, far_off(*sums), outs, scratch, cost=(1000, 4 * ka.size), after=after)


def fold_last(sums, docs, after=()):
    ka, _, kb, _ = sums
    r = ka.shape[0] // docs
    na, nb = ka.shape[1], kb.shape[1]

    def body(ins, outs):
        a, ga, b, gb = ins
        (out,) = outs
        for d in range(docs):
            at = slice(d * r, (d + 1) * r)
            out[d, :, :na] = (a[at].astype(f32) + ga[at].astype(f32)).astype(bf16)
            out[d, :, na:] = (b[at].astype(f32) + gb[at].astype(f32)).astype(bf16)

    return call(
        body, far_off(*sums), [((docs, r, na + nb), bf16)], cost=(1000, 4 * ka.size), after=after
    )[0]


def pack_small(smalls, biases, convs, after=()):
    layers = len(smalls)
    width = smalls[0].shape[1]
    ff = biases[0].shape[1]
    nv, nb = 4 * width // 128, ff // 128
    rows = nv + nb + 40

    def body(ins, outs):
        (out_ref,) = outs
        _, core = place()
        r = lax.broadcasted_iota(jnp.int32, (width, 128), 0) // HEAD_DIM
        c = lax.broadcasted_iota(jnp.int32, (width, 128), 1)
        head = r + (HEADS // 2) * core
        head = jnp.where(head >= HEADS, head - HEADS, head)
        hot = jnp.where(head == c, 1.0, 0.0).astype(bf16)
        for layer in range(layers):
            s_ref, b_ref, c_ref = ins[3 * layer : 3 * layer + 3]
            for j in range(width // 128):
                for k in range(4):
                    out_ref[layer, k * (width // 128) + j : k * (width // 128) + j + 1] = (
                        s_ref[k : k + 1, 128 * j : 128 * (j + 1)]
                    )
            for j in range(nb):
                lane = slice(128 * j, 128 * (j + 1))
                oth = 128 * ((j + nb // 2) % nb)
                piece = jnp.where(core == 0, b_ref[:, lane], b_ref[:, oth : oth + 128])
                out_ref[layer, nv + j : nv + j + 1] = piece
            c1, c2, c3 = split3(c_ref[...])
            out_ref[layer, nv + nb :] = dg(c1, hot, NN) + (dg(c2, hot, NN) + dg(c3, hot, NN))

    ins = [x for layer in range(layers) for x in (smalls[layer], biases[layer], convs[layer])]
    return call(body, ins, [((layers, rows, 128), f32, None)], after=after)[0]


def partner(x, axis, mask):
    n = lax.axis_size(axis)
    return lax.ppermute(x, axis, [(i, i ^ mask) for i in range(n)])


def swap(x):
    return partner(x, "core", 1)


def sum_over(x, axis):
    n = lax.axis_size(axis)
    if n <= 4:
        parts = [partner(x, axis, m) for m in range(1, n)]
        for p in parts:
            x = x + p
        return x
    bit = 1
    while bit < n:
        x = x + partner(x, axis, bit)
        bit *= 2
    return x


def total_and_other(keep, send):
    parts = lax.axis_size("part")
    mine = keep + swap(send)
    got = exchange(jnp.broadcast_to(mine[None], (parts, *mine.shape)), "part")
    total = got[0]
    for p in range(1, parts):
        total = total + got[p]
    return total, swap(total)


def exchange(x, axes):
    return lax.all_to_all(x, axes, 0, 0, tiled=True)


def rims(tails, heads):
    n = 2 * lax.axis_size("part")
    axes = ("part", "core")
    return (
        lax.ppermute(tails, axes, [(i, (i + 1) % n) for i in range(n)]),
        lax.ppermute(heads, axes, [((i + 1) % n, i) for i in range(n)]),
    )


def halve_parts(keep, got, n, low_first):
    me = lax.axis_index("part")
    parts = lax.axis_size("part")
    docs = lax.axis_size("doc")
    cols = keep.shape[1]
    bit = parts // n if low_first else n // 2
    while n > 1:
        shape = (docs, n // 2, 2, -1, cols) if low_first else (docs, 2, n // 2, -1, cols)
        axis = 2 if low_first else 1
        mine = (me // bit) % 2
        k, g = keep.reshape(shape), got.reshape(shape)
        pick = lambda x, i: lax.dynamic_index_in_dim(x, i, axis, keepdims=False).astype(f32)
        send = (pick(k, 1 - mine) + pick(g, 1 - mine)).astype(bf16)
        keep = (pick(k, mine) + pick(g, mine)).astype(bf16)
        got = partner(send, "part", bit)
        n //= 2
        bit = bit * 2 if low_first else bit // 2
    return (keep.astype(f32) + got.astype(f32)).astype(bf16).reshape(docs, -1, cols)


def first_halves(outs):
    parts = lax.axis_size("part")
    docs = lax.axis_size("doc")
    if len(outs) == 2:
        pieces = []
        for x, low_first in zip(outs, (True, False)):
            bit = 1 if low_first else parts // 2
            shape = (docs, parts // 2, 2, -1, x.shape[1]) if low_first else (
                docs, 2, parts // 2, -1, x.shape[1])
            axis = 2 if low_first else 1
            mine = (lax.axis_index("part") // bit) % 2
            v = x.reshape(shape)
            for i in (mine, 1 - mine):
                pieces.append(
                    lax.dynamic_index_in_dim(v, i, axis, keepdims=False).reshape(-1, x.shape[1])
                )
        outs = pieces
    ka, sa, kb, sb = outs
    return ka, partner(sa, "part", 1), kb, partner(sb, "part", parts // 2)


def second_halves(sums, after=()):
    parts = lax.axis_size("part")
    docs = lax.axis_size("doc")
    if parts == 4 and sums[0].shape[0] // (2 * docs) % 16 == 0:
        ka, sa, kb, sb = fold(sums, docs, parts, after)
        return ka, partner(sa, "part", 2), kb, partner(sb, "part", 1)
    out = []
    for keep, got, low_first in ((*sums[:2], True), (*sums[2:], False)):
        x = halve_parts(keep, got, parts // 2, low_first).reshape(-1, keep.shape[1])
        out += [x, jnp.zeros_like(x)]
    return tuple(out)


def third(sums, after=()):
    docs = lax.axis_size("doc")
    if sums[0].shape[0] // docs % 16 == 0:
        x = fold_last(sums, docs, after)
    else:
        ka, ga, kb, gb = (x.reshape(docs, -1, x.shape[1]) for x in sums)
        x = jnp.concatenate([ka + ga, kb + gb], axis=2)
    return x


def finish(feeds, att):
    layers = len(feeds)
    docs, r, nf = feeds[0].shape
    half = att.shape[2] // (3 * layers)
    ffh = (nf - half) // 2

    def body(ins, outs):
        q_ref, k_ref, v_ref, o_ref, u_ref, d_ref = outs

        def total(ref, at, size):
            s = ref[0, :, at : at + size].astype(f32)
            for d in range(1, docs):
                s = s + ref[d, :, at : at + size].astype(f32)
            return s

        for layer in reversed(range(layers)):
            ff = ins[layers - 1 - layer]
            u_ref[layer] = total(ff, 0, ffh)
            o_ref[layer] = total(ff, ffh, half).T
            for j in range(ffh // half):
                d_ref[layer, j * half : (j + 1) * half] = total(ff, ffh + half + j * half, half).T
        for layer in range(layers):
            for j, ref in enumerate((q_ref, k_ref, v_ref)):
                ref[layer] = total(ins[layers], (3 * layer + j) * half, half)

    ins = far_off(*reversed(feeds), att)
    outs = [((layers, r, half), f32)] * 3 + [
        ((layers, half, r), f32), ((layers, r, ffh), f32), ((layers, ffh, r), f32)
    ]
    return call(body, ins, outs)


def local(inputs, cotangent, lengths, query_weight, key_weight, value_weight, conv_weight,
          out_weight, gain_one, shift_one, up_weight, up_bias, down_weight, gain_two, shift_two):
    docs, chunk, width = inputs.shape
    parts = lax.axis_size("part")
    doc, part, core = (lax.axis_index(a) for a in ("doc", "part", "core"))
    half = query_weight.shape[2]
    ffh = up_weight.shape[2]
    rows = docs * chunk
    group = ("part", "core")

    state = exchange(inputs, "doc").reshape(rows, width)
    wqkv = jnp.concatenate([query_weight, key_weight, value_weight], axis=2)
    wqkv = (wqkv, swap(wqkv))

    length = lengths[doc]
    place = ((jnp.arange(docs, dtype=jnp.int32) * parts + part) * 2 + core) * chunk
    place = (place[:, None] + jnp.arange(chunk, dtype=jnp.int32)[None, :]).reshape(rows)
    valid = (place < length).astype(f32)[:, None]
    bounds = jnp.arange(LANDMARKS + 1, dtype=jnp.int32) * length // LANDMARKS
    inside = (
        (place[:, None] >= bounds[None, :-1]) & (place[:, None] < bounds[None, 1:])
    ).astype(bf16)
    icounts = 1.0 / (bounds[1:] - bounds[:-1]).astype(f32)[:, None]

    xbar = dg(inside, state, TN)
    first = core == 0
    keep = jnp.where(first, xbar[:, : width // 2], xbar[:, width // 2 :])
    send = jnp.where(first, xbar[:, width // 2 :], xbar[:, : width // 2])
    wo = (out_weight, swap(out_weight))
    wu = (up_weight, swap(up_weight))
    wd = (down_weight, swap(down_weight))
    bias = jnp.concatenate([up_bias, swap(up_bias)], axis=1)
    conv = jnp.concatenate([conv_weight, swap(conv_weight)], axis=1)
    taps = prepare_taps(jnp.pad(conv, ((0, 0), (0, 16 - HEADS), (0, 40 - TAPS))))
    grad = exchange(cotangent, "doc").reshape(rows, width)

    low = state
    low_got = swap(state)
    kept = []
    for layer in range(LAYERS):
        xtot, xoth = total_and_other(keep, send)
        qkv, tails, heads = project(
            low, wqkv, valid, layer, docs, after=(grad, wo[1], wu[1], wd[1]) if layer == 0 else ()
        )
        vprev, vnext = rims(tails, heads)
        ne, marks, qk, pieces = scores(
            qkv, xtot, xoth, icounts, wqkv, valid, layer, parts
        )
        inv, end = inverse(qk)
        merged, summary = merge(exchange(pieces, group), end)
        mixed, pack, own, rr, dgelu, nxt_state, nxt_low, keep, send = forward_rows(
            ne, exchange(merged, group), qkv, vprev, vnext, taps, state,
            (wo, wu, wd, bias[layer : layer + 1]), (gain_one, shift_one, gain_two, shift_two),
            valid, inside, layer,
        )
        pack_got = swap(pack)
        kept.append(dict(
            low=(low, low_got), qkv=qkv, vprev=vprev, vnext=vnext, ne=ne, marks=marks,
            inv=inv, summary=summary, mixed=mixed, pack=(pack, pack_got), own=own, rr=rr,
            dgelu=dgelu,
        ))
        state, low = nxt_state, nxt_low
        at = width + half + ffh
        low_got = lanes_of(pack_got, at, width)
        kept[-1]["next_low"] = (lanes_of(pack, at, width), low_got)
    output = exchange(state.reshape(docs, chunk, width), "doc")

    smalls, biases, convs = [None] * LAYERS, [None] * LAYERS, [None] * LAYERS
    ff_sums = None
    att_args = []
    for layer in reversed(range(LAYERS)):
        s = kept[layer]
        pack, gu, gbias, gr1, gatt, gqn, pieces, small, tails, heads = backward_rows(
            grad, s["rr"], s["dgelu"], s["ne"], s["mixed"], s["qkv"], s["marks"],
            (wo, wu, wd), (gain_one, gain_two), valid, layer, docs, parts,
            after=() if ff_sums is None else (output,),
        )
        pieces = exchange(pieces, group)
        gprev, gnext = rims(tails, heads)
        pack_got = swap(pack)
        before = (gprev, gnext)
        if ff_sums is not None:
            ff_sums = second_halves(ff_sums, after=(small,))
            before = (gprev, gnext, ff_sums[0])
        pulled = inverse_pull(pieces, s["summary"], s["inv"], after=before)
        got = exchange(pulled, group)
        gvc, cg = conv_pull(
            s["qkv"], gatt, gprev, gnext, s["vprev"], s["vnext"], taps, layer, after=(pulled,)
        )
        gk, gv, gmid, gown, goth = far_pull(
            s["ne"], s["marks"], s["mixed"], got, s["qkv"], gvc, inside, icounts, valid,
        )
        gown, goth = total_and_other(gown, goth)
        fpack, fpack_got = s["pack"]
        arrays = [(pack, None), (pack_got, None), (gu, None), lanes_of(fpack, 0, width),
                  lanes_of(fpack_got, 0, width + half + ffh), (s["own"], None)]
        lefts = [((3, 0), (4, 0), width), ((0, 0), (1, 0), width), ((0, width), (1, width), width)]
        rights = [((2, 0), (1, 2 * width)), ((5, half), (4, width + half)), ((5, 0), (4, width))]
        nt = ffh // 384
        tiles = [(0, 0, j, 0) for j in range(nt)] + [(2, 2, 0, 0)] + [(1, 1, j, 1) for j in range(nt)]
        sums = weight_grads(arrays, lefts, rights, tiles, docs, parts, after=(gk,))
        before = (sums[0],)
        if ff_sums is not None:
            ff_above = third(ff_sums, after=before)
            before = (ff_above,)
            ff_above = exchange(ff_above, "doc")
        qkv, qkv_send, grad = input_pull(
            gqn, gown, goth, gmid, inside, icounts, gk, gv, gr1, wqkv, layer,
            f32 if layer > 0 else bf16, after=before,
        )
        qkv_got = swap(qkv_send)
        ff_sums = first_halves(sums)
        low_pair = s["low"] if layer == 0 else kept[layer - 1]["next_low"]
        low, low_got = low_pair if isinstance(low_pair[0], tuple) else far_off(*low_pair)
        att_args.append([low, low_got, (qkv, None), (qkv_got, None)])
        smalls[layer], biases[layer], convs[layer] = small, gbias, cg
    att_args.reverse()
    att = weight_grads(
        [x for args in att_args for x in args],
        [((4 * l, 0), (4 * l + 1, 0), width) for l in range(LAYERS)],
        [((4 * l + 2, 0), (4 * l + 3, 0)) for l in range(LAYERS)],
        [(l, l, j, l) for l in range(LAYERS) for j in range(3)], docs, parts,
    )
    grad_inputs = exchange(grad.reshape(docs, chunk, width), "doc")
    ff_sums = second_halves(ff_sums, after=(att[0], ff_above))
    att = second_halves(first_halves(att), after=(ff_sums[0], grad_inputs))
    small = pack_small(smalls, biases, convs, after=(ff_sums[0],))
    small = sum_over(small + swap(small), "part")
    ff_now = third(ff_sums, after=(att[0], small))
    small = sum_over(small, "doc")
    att = third(att, after=(ff_now, small))
    ff_now, att = exchange(ff_now, "doc"), exchange(att, "doc")
    grad_inputs = grad_inputs.astype(f32)

    nv = width // 128
    vec = [small[:, i * nv : (i + 1) * nv].reshape(LAYERS, width) for i in range(4)]
    nb = 2 * ffh // 128
    gbias = small[:, 4 * nv : 4 * nv + nb].reshape(LAYERS, 2 * ffh)
    gconv = jnp.swapaxes(small[:, 4 * nv + nb : 4 * nv + nb + TAPS, :HEADS], 1, 2)
    q, k, v, o, u, d = finish([ff_now, ff_above], att)
    return (
        output, grad_inputs, q, k, v, gconv, o, vec[0], vec[1], u, gbias, d, vec[2], vec[3],
    )


def solution(mesh):
    seq = ("doc", "part")
    rows = P(None, ("doc", "part", "core"), None)
    placed = (
        rows, rows, P(), P(None, None, "core"), P(None, None, "core"), P(None, None, "core"),
        P(None, "core", None), P(None, "core", None), P(), P(), P(None, None, "core"),
        P(None, "core"), P(None, "core", None), P(), P(),
    )
    outs = (
        rows, rows, P(None, seq, "core"), P(None, seq, "core"), P(None, seq, "core"), P(),
        P(None, "core", seq), P(), P(), P(None, seq, "core"), P(), P(None, "core", seq), P(), P(),
    )

    def run(*args):
        docs = args[0].shape[0]
        seq_size = mesh.shape["seq"]
        cut = Mesh(
            mesh.devices.reshape(docs, seq_size // docs, mesh.shape["head"]),
            ("doc", "part", "core"),
        )
        return jax.shard_map(local, mesh=cut, in_specs=placed, out_specs=outs, check_vma=False)(*args)

    return run
```

time: 687 us -> 539 us (0.78)
  local copies, waits for them, and re-layouts: 102 us -> 27.7 us
  Pallas kernels: 160 us -> 218 us
  starting transfers between devices: 152 us -> 106 us
  other arithmetic: 45.9 us -> 3.83 us
  waiting for transfers between devices: 154 us -> 127 us
  matrix products: 16.4 us -> 0.3 us
    ppermute x123 -> x40, waiting for transfers between devices: 151 us -> 34.9 us  [partner(): return lax.ppermute(x, axis, [(i, i ^ mask) for i in range(n)])]
    ppermute x123 -> x40, starting transfers between devices: 125 us -> 28.7 us  [partner(): return lax.ppermute(x, axis, [(i, i ^ mask) for i in range(n)])]
    all_to_all x4 -> x16, waiting for transfers between devices: 0.01 us -> 72.3 us  [exchange(): return lax.all_to_all(x, axes, 0, 0, tiled=True)]
    pallas_call x18 -> x32, Pallas kernels: 160 us -> 218 us  [call(): pl.pallas_call(kernel, out_shape=[jax.ShapeDtypeStruct(shape, t) for shap...]
    all_to_all x4 -> x16, starting transfers between devices: 15.9 us -> 66.1 us  [exchange(): return lax.all_to_all(x, axes, 0, 0, tiled=True)]
    all_to_all x0 -> x3, blocking collectives: none -> 44.8 us  [exchange(): return lax.all_to_all(x, axes, 0, 0, tiled=True)]
    all_gather x4 -> x0, blocking collectives: 41.9 us -> none  [from_owners(): got = lax.all_gather(x, ('part', 'core'), axis=0)]
    slice x110 -> x0, local copies, waits for them, and re-layouts: 28.7 us -> none  [the longest x12 11 us: both_own(): return jnp.concatenate([x[:, :half], swap(x[:, half:])], axis=0)]
  transfers between devices with their start and end apart: 135 -> 64, of which waited for: 49 -> 22; matrix products, arithmetic and copies ran while one was open for 22% -> 3% of each run, Pallas kernels for 21% -> 29%
where the time goes in v1:
time: 539 us; the launch traced here: 529 us
  Pallas kernels  218 us (40%)
  waiting for transfers between devices  127 us (24%)
  starting transfers between devices  106 us (20%)
  blocking collectives  44.8 us (8%)
  local copies, waits for them, and re-layouts  27.7 us (5%)
    pallas_call x32, Pallas kernels, call(): pl.pallas_call(kernel, out_shape=[jax.ShapeDtypeStruct(shape, t) for shap...  218 us
    all_to_all x16, waiting for transfers between devices, exchange(): return lax.all_to_all(x, axes, 0, 0, tiled=True)  72.3 us
    all_to_all x16, starting transfers between devices, exchange(): return lax.all_to_all(x, axes, 0, 0, tiled=True)  66.1 us
    all_to_all x3, blocking collectives, exchange(): return lax.all_to_all(x, axes, 0, 0, tiled=True)  44.8 us
    ppermute x40, waiting for transfers between devices, partner(): return lax.ppermute(x, axis, [(i, i ^ mask) for i in range(n)])  34.9 us
    ppermute x40, starting transfers between devices, partner(): return lax.ppermute(x, axis, [(i, i ^ mask) for i in range(n)])  28.7 us
    unnamed x73, local copies, waits for them, and re-layouts  22.7 us
    ppermute x4, waiting for transfers between devices, rims(): lax.ppermute(tails, axes, [(i, (i + 1) % n) for i in range(n)])  19.4 us
  transfers between devices with their start and end apart: 64, of which 22 were waited for; matrix products, arithmetic and copies ran while one was open for 3% of the time, Pallas kernels for 29%

profile of v1, /device:TPU:0, one launch (start us, length us, event | category | flops | bytes accessed | tf_op | source)
XLA Modules:
  0.0 528.7 jit_solution(17975139771150378282)
XLA Ops:
  7.1 5.9 %all-to-all-start = ((bf16[4,64,768]{2,1,0:T(8,128)(2,1)}), bf16[4,64,768]{2,1,0:T(8,128)(2,1)S(1)}, u32[]{:S(2)}, u32[]{:S(2)}) async-start(bf16[4,64,768]{2,1,0:T(8,128)(2,1)} %param.15), calls=%async_computation | async-start | bytes 786432 | tf_op jit(solution)/shard_map/all_to_all | solution.py:1000
  14.6 10.8 %all-to-all-done = bf16[4,64,768]{2,1,0:T(8,128)(2,1)S(1)} async-done(((bf16[4,64,768]{2,1,0:T(8,128)(2,1)}), bf16[4,64,768]{2,1,0:T(8,128)(2,1)S(1)}, u32[]{:S(2)}, u32[]{:S(2)}) %all-to-all-start) | async-done | bytes 393248 | tf_op jit(solution)/shard_map/all_to_all | solution.py:1000
  32.4 6.4 %all-to-all-done.2 = f32[4,64,384]{2,1,0:T(8,128)S(1)} async-done(((f32[4,64,384]{2,1,0:T(8,128)}), f32[4,64,384]{2,1,0:T(8,128)S(1)}, u32[]{:S(2)}, u32[]{:S(2)}) %all-to-all-start.2) | async-done | bytes 393248 | tf_op jit(solution)/shard_map/all_to_all | solution.py:1000
  44.0 9.6 %all-to-all-done.1 = bf16[4,64,768]{2,1,0:T(8,128)(2,1)S(1)} async-done(((bf16[4,64,768]{2,1,0:T(8,128)(2,1)}), bf16[4,64,768]{2,1,0:T(8,128)(2,1)S(1)}, u32[]{:S(2)}, u32[]{:S(2)}) %all-to-all-start.1) | async-done | bytes 393248 | tf_op jit(solution)/shard_map/all_to_all | solution.py:1000
  53.7 4.9 shard_map.254
  58.6 8.3 %shard_map.256 = (f32[256,1536]{1,0:T(8,128)}, f32[72,1536]{1,0:T(8,128)S(1)}, f32[128,128]{1,0:T(8,128)S(1)}, f32[8,72,128]{2,1,0:T(8,128)}) custom-call(f32[64,384]{1,0:T(8,128)S(1)} %fusion.5.refs_0_, f32[64,384]{1,0:T(8,128)S(1)} %collective-permute-done.8.refs_1_, f32[64,1]{1,0:T(8,128)S(1)} %copy.43.refs_2_.refs_3_.refs_10_, ...), custom_call_target="tpu_custom_call" | custom-call | flops 905969664 | bytes 7864320 | tf_op jit(solution)/shard_map/pallas_call | solution.py:279
  73.1 6.1 %shard_map.257 = (f32[27,128,128]{2,1,0:T(8,128)S(1)}, f32[128,128]{1,0:T(8,128)S(1)}) custom-call(f32[128,128]{1,0:T(8,128)S(1)} %get-tuple-element.125.refs_0_), custom_call_target="tpu_custom_call" | custom-call | flops 2516582400 | bytes 1703936 | tf_op jit(solution)/shard_map/pallas_call | solution.py:279
  85.7 7.2 %all-to-all-done.4.refs_4_ = f32[8,72,128]{2,1,0:T(8,128)S(1)} async-done(((f32[8,72,128]{2,1,0:T(8,128)}), f32[8,72,128]{2,1,0:T(8,128)S(1)}, u32[]{:S(2)}, u32[]{:S(2)}) %all-to-all-start.4) | async-done | bytes 294944 | tf_op jit(solution)/shard_map/all_to_all | solution.py:1000
  92.8 16.2 %shard_map.259 = (f32[72,768]{1,0:T(8,128)S(1)}, bf16[256,3456]{1,0:T(8,128)(2,1)}, bf16[256,1920]{1,0:T(8,128)(2,1)}, f32[256,1536]{1,0:T(8,128)}, bf16[256,307...) custom-call(f32[256,2304]{1,0:T(8,128)} %get-tuple-element.121.refs_, ...), custom_call_target="tpu_custom_call" | custom-call | flops 5435817984 | bytes 23592960 | tf_op jit(solution)/shard_map/pallas_call | solution.py:279
  110.5 10.5 %all_to_all.95 = f32[4,64,384]{2,1,0:T(8,128)S(1)} all-to-all(f32[4,64,384]{2,1,0:T(8,128)S(1)} %broadcast_in_dim.9), channel_id=1, replica_groups=mesh['doc'=4,'part'=4,'core'=2] {'part'}, dimensions={0} | all-to-all | bytes 786432 | tf_op jit(solution)/shard_map/all_to_all | solution.py:1000
  121.1 4.9 shard_map.260
  126.1 8.4 %shard_map.261 = (f32[256,1536]{1,0:T(8,128)}, f32[72,1536]{1,0:T(8,128)S(1)}, f32[128,128]{1,0:T(8,128)S(1)}, f32[8,72,128]{2,1,0:T(8,128)}) custom-call(f32[64,384]{1,0:T(8,128)S(1)} %fusion.4.refs_0_, f32[64,384]{1,0:T(8,128)S(1)} %collective-permute-done.13.refs_1_, f32[64,1]{1,0:T(8,128)S(1)} %copy.43.refs_2_.refs_3_.refs_10_, ...), custom_call_target="tpu_custom_call" | custom-call | flops 905969664 | bytes 7864320 | tf_op jit(solution)/shard_map/pallas_call | solution.py:279
  138.0 6.1 %shard_map.262 = (f32[27,128,128]{2,1,0:T(8,128)S(1)}, f32[128,128]{1,0:T(8,128)S(1)}) custom-call(f32[128,128]{1,0:T(8,128)S(1)} %get-tuple-element.136.refs_0_), custom_call_target="tpu_custom_call" | custom-call | flops 2516582400 | bytes 1703936 | tf_op jit(solution)/shard_map/pallas_call | solution.py:279
  146.8 4.1 all-to-all-start.7
  153.7 8.3 %collective-permute-done.10.refs_1_ = f32[64,768]{1,0:T(8,128)S(1)} collective-permute-done((f32[64,768]{1,0:T(8,128)}, f32[64,768]{1,0:T(8,128)S(1)}, u32[]{:S(2)}, u32[]{:S(2)}) %collective-permute-start.10) | collective-permute-done | bytes 196640 | tf_op jit(solution)/shard_map/ppermute | solution.py:1007
  162.0 16.7 %shard_map.264 = (f32[72,768]{1,0:T(8,128)S(1)}, bf16[256,3456]{1,0:T(8,128)(2,1)}, bf16[256,1920]{1,0:T(8,128)(2,1)}, f32[256,1536]{1,0:T(8,128)}, bf16[256,307...) custom-call(f32[256,2304]{1,0:T(8,128)} %get-tuple-element.130.refs_, ...), custom_call_target="tpu_custom_call" | custom-call | flops 5435817984 | bytes 23592960 | tf_op jit(solution)/shard_map/pallas_call | solution.py:279
  178.7 12.6 %shard_map.265 = (bf16[256,3072]{1,0:T(8,128)(2,1)}, bf16[256,1536]{1,0:T(8,128)(2,1)}, f32[1,3072]{1,0:T(1,128)S(1)}, f32[256,768]{1,0:T(8,128)}, f32[256,768]{...) custom-call(bf16[256,768]{1,0:T(8,128)(2,1)S(1)} %bitcast.45, ...), custom_call_target="tpu_custom_call" | custom-call | flops 5435817984 | bytes 23592960 | tf_op jit(solution)/shard_map/pallas_call | solution.py:279
  192.0 4.1 all-to-all-start.9
  199.1 10.5 %collective-permute-done.14.refs_3_.refs_5_ = f32[64,768]{1,0:T(8,128)S(1)} collective-permute-done((f32[64,768]{1,0:T(8,128)}, f32[64,768]{1,0:T(8,128)S(1)}, u32[]{:S(2)}, u32[]{:S(2)}) %collective-permute-start.14) | collective-permute-done | bytes 196640 | tf_op jit(solution)/shard_map/ppermute | solution.py:1007
  209.6 9.9 %shard_map.266.refs_7_ = f32[8,200,128]{2,1,0:T(8,128)} custom-call(f32[64,128]{1,0:T(8,128)S(1)} %get-tuple-element.147.refs_0_, f32[8,128,128]{2,1,0:T(8,128)} %all-to-all-done.9.refs_1_, f32[27,128,128]{2,1,0:T(8,128)} %copy-done.23, f32[64,768]{1,0:T(8,128)S(1)} %collective-permute-done.14.refs_3_.refs_5_, ...), custom_call_target="tpu_custom_call" | custom-call | flops 5234491392 | bytes 1703936 | tf_op jit(solution)/shard_map/pallas_call | solution.py:279
  219.5 4.2 all-to-all-start.10
  224.1 8.8 %shard_map.267 = (f32[256,768]{1,0:T(8,128)S(1)}, f32[40,768]{1,0:T(8,128)S(1)}) custom-call(f32[256,2304]{1,0:T(8,128)} %get-tuple-element.130.refs_6_.refs_7_.refs_0_.refs_15_.refs_5_, f32[64,768]{1,0:T(8,128)S(1)} %collective-permute-done.10.refs_1_, f32[64,768]{1,0:T(8,128)S(1)} %collective-permute-done.11.refs_2_, ...), custom_call_target="tpu_custom_call" | custom-call | flops 519045120 | bytes 3145728 | tf_op jit(solution)/shard_map/pallas_call | solution.py:279
  236.7 6.1 %shard_map.268 = (bf16[256,768]{1,0:T(8,128)(2,1)S(1)}, bf16[256,768]{1,0:T(8,128)(2,1)S(1)}, f32[64,768]{1,0:T(8,128)S(1)}, f32[64,384]{1,0:T(8,128)S(1)}, f32[64,384]{1,0:T(8,128)S(1)}) custom-call(f32[8,200,128]{2,1,0:T(8,128)} %all-to-all-done.10.refs_0_, f32[72,768]{1,0:T(8,128)S(1)} %get-tuple-element.144.refs_13_.refs_1_, ...), custom_call_target="tpu_custom_call" | custom-call | flops 1509949440 | bytes 9437184 | tf_op jit(solution)/shard_map/pallas_call | solution.py:279
  244.3 10.1 %all_to_all.96 = f32[4,64,384]{2,1,0:T(8,128)S(1)} all-to-all(f32[4,64,384]{2,1,0:T(8,128)S(1)} %broadcast_in_dim.10), channel_id=1, replica_groups=mesh['doc'=4,'part'=4,'core'=2] {'part'}, dimensions={0} | all-to-all | bytes 786432 | tf_op jit(solution)/shard_map/all_to_all | solution.py:1000
  254.4 4.6 all-to-all-start.8
  260.1 11.0 %shard_map.269 = (bf16[384,1920]{1,0:T(8,128)(2,1)}, bf16[384,1920]{1,0:T(8,128)(2,1)}, bf16[384,1536]{1,0:T(8,128)(2,1)}, bf16[384,1536]{1,0:T(8,128)(2,1)}) custom-call(bf16[256,3072]{1,0:T(8,128)(2,1)} %get-tuple-element.160.refs_0_, bf16[256,3072]{1,0:T(8,128)(2,1)} %collective-permute-done.18.refs_1_, bf16[256,1536]{1,0:T(8,128)(2,1)S(1)} %copy-done.14, ...), custom_call_target="tpu_custom_call" | custom-call | flops 2717908992 | bytes 5308416 | tf_op jit(solution)/shard_map/pallas_call | solution.py:279
  274.1 5.9 %shard_map.270 = (bf16[256,1152]{1,0:T(8,128)(2,1)S(1)}, bf16[256,1152]{1,0:T(8,128)(2,1)}, f32[256,768]{1,0:T(8,128)}) custom-call(f32[256,768]{1,0:T(8,128)} %get-tuple-element.146.refs_0_, bf16[256,768]{1,0:T(8,128)(2,1)S(1)} %get-tuple-element.154.refs_6_.refs_1_, bf16[256,768]{1,0:T(8,128)(2,1)S(1)} %get-tuple-element.155.refs_2_, ...), custom_call_target="tpu_custom_call" | custom-call | flops 905969664 | bytes 6291456 | tf_op jit(solution)/shard_map/pallas_call | solution.py:279
  280.9 13.8 %shard_map.271 = (bf16[256,3072]{1,0:T(8,128)(2,1)}, bf16[256,1536]{1,0:T(8,128)(2,1)}, f32[1,3072]{1,0:T(1,128)S(1)}, f32[256,768]{1,0:T(8,128)}, f32[256,768]{...) custom-call(f32[256,768]{1,0:T(8,128)} %get-tuple-element.165.refs_0, ...), custom_call_target="tpu_custom_call" | custom-call | flops 5435817984 | bytes 23592960 | tf_op jit(solution)/shard_map/pallas_call | solution.py:279
  301.2 5.5 %collective-permute-done.22.refs_1_ = bf16[384,1920]{1,0:T(8,128)(2,1)} collective-permute-done((bf16[384,1920]{1,0:T(8,128)(2,1)}, bf16[384,1920]{1,0:T(8,128)(2,1)}, u32[]{:S(2)}, u32[]{:S(2)}) %collective-permute-start.22) | collective-permute-done | bytes 1474592 | tf_op jit(solution)/shard_map/ppermute | solution.py:968
  306.8 4.4 shard_map.272
  313.4 8.9 %shard_map.273.refs_7_ = f32[8,200,128]{2,1,0:T(8,128)} custom-call(f32[64,128]{1,0:T(8,128)S(1)} %get-tuple-element.171.refs_0_, f32[8,128,128]{2,1,0:T(8,128)S(1)} %all-to-all-done.12.refs_1_, f32[27,128,128]{2,1,0:T(8,128)} %copy-done.22, f32[64,768]{1,0:T(8,128)S(1)} %collective-permute-done.20.refs_3_.refs_5_, ...), custom_call_target="tpu_custom_call" | custom-call | flops 5234491392 | bytes 1703936 | tf_op jit(solution)/shard_map/pallas_call | solution.py:279
  322.3 4.6 all-to-all-start.13
  330.5 8.8 %shard_map.274 = (f32[256,768]{1,0:T(8,128)S(1)}, f32[40,768]{1,0:T(8,128)S(1)}) custom-call(f32[256,2304]{1,0:T(8,128)} %get-tuple-element.121.refs_6_.refs_7_.refs_0_.refs_15_.refs_5_, f32[64,768]{1,0:T(8,128)S(1)} %collective-permute-done.4.refs_1_, f32[64,768]{1,0:T(8,128)S(1)} %collective-permute-done.5.refs_2_, f32[256,768]{1,0:T(8,128)} %get-tuple-element.181.refs_3_, ...), custom_call_target="tpu_custom_call" | custom-call | flops 519045120 | bytes 3145728 | tf_op jit(solution)/shard_map/pallas_call | solution.py:279
  340.4 6.1 %shard_map.275 = (bf16[256,768]{1,0:T(8,128)(2,1)S(1)}, bf16[256,768]{1,0:T(8,128)(2,1)S(1)}, f32[64,768]{1,0:T(8,128)S(1)}, f32[64,384]{1,0:T(8,128)S(1)}, f32[64,384]{1,0:T(8,128)S(1)}) custom-call(f32[8,200,128]{2,1,0:T(8,128)} %all-to-all-done.13.refs_0_, f32[72,768]{1,0:T(8,128)S(1)} %get-tuple-element.168.refs_13_.refs_1_, ...), custom_call_target="tpu_custom_call" | custom-call | flops 1509949440 | bytes 9437184 | tf_op jit(solution)/shard_map/pallas_call | solution.py:279
  348.7 4.6 all-to-all-start.14
  354.4 11.0 %shard_map.276 = (bf16[384,1920]{1,0:T(8,128)(2,1)}, bf16[384,1920]{1,0:T(8,128)(2,1)}, bf16[384,1536]{1,0:T(8,128)(2,1)}, bf16[384,1536]{1,0:T(8,128)(2,1)}) custom-call(bf16[256,3072]{1,0:T(8,128)(2,1)} %get-tuple-element.192.refs_0_, bf16[256,3072]{1,0:T(8,128)(2,1)} %collective-permute-done.28.refs_1_, bf16[256,1536]{1,0:T(8,128)(2,1)S(1)} %copy-done.13, ...), custom_call_target="tpu_custom_call" | custom-call | flops 2717908992 | bytes 5308416 | tf_op jit(solution)/shard_map/pallas_call | solution.py:279
  368.8 4.7 all-to-all-start.16
  378.6 6.2 %shard_map.278 = (bf16[256,1152]{1,0:T(8,128)(2,1)}, bf16[256,1152]{1,0:T(8,128)(2,1)}, bf16[256,768]{1,0:T(8,128)(2,1)}) custom-call(f32[256,768]{1,0:T(8,128)} %get-tuple-element.170.refs_0_, bf16[256,768]{1,0:T(8,128)(2,1)S(1)} %get-tuple-element.183.refs_6_.refs_1_, bf16[256,768]{1,0:T(8,128)(2,1)S(1)} %get-tuple-element.184.refs_2_, ...), custom_call_target="tpu_custom_call" | custom-call | flops 905969664 | bytes 6291456 | tf_op jit(solution)/shard_map/pallas_call | solution.py:279
  389.3 6.6 %shard_map.279 = (bf16[384,1152]{1,0:T(8,128)(2,1)}, bf16[384,1152]{1,0:T(8,128)(2,1)}, bf16[384,1152]{1,0:T(8,128)(2,1)}, bf16[384,1152]{1,0:T(8,128)(2,1)}) custom-call(bf16[256,768]{1,0:T(8,128)(2,1)S(1)} %bitcast.43, bf16[256,768]{1,0:T(8,128)(2,1)S(1)} %collective-permute-done.32.refs_1_, bf16[256,1152]{1,0:T(8,128)(2,1)S(1)} %copy-done.18, ...), custom_call_target="tpu_custom_call" | custom-call | flops 1811939328 | bytes 3538944 | tf_op jit(solution)/shard_map/pallas_call | solution.py:279
  397.3 8.3 %all-to-all-done.16.refs_5_.refs_0_ = bf16[4,48,3456]{2,1,0:T(8,128)(2,1)} async-done(((bf16[4,48,3456]{2,1,0:T(8,128)(2,1)}), bf16[4,48,3456]{2,1,0:T(8,128)(2,1)}, u32[]{:S(2)}, u32[]{:S(2)}) %all-to-all-start.16) | async-done | bytes 1327136 | tf_op jit(solution)/shard_map/all_to_all | solution.py:1000
  409.3 4.8 shard_map.280
  419.6 10.1 %collective-permute-done.40 = f32[2,88,128]{2,1,0:T(8,128)S(1)} collective-permute-done((f32[2,88,128]{2,1,0:T(8,128)S(1)}, f32[2,88,128]{2,1,0:T(8,128)S(1)}, u32[]{:S(2)}, u32[]{:S(2)}) %collective-permute-start.40) | collective-permute-done | bytes 90144 | tf_op jit(solution)/shard_map/ppermute | solution.py:968
  442.2 5.7 %collective-permute-done.46 = f32[2,88,128]{2,1,0:T(8,128)S(1)} collective-permute-done((f32[2,88,128]{2,1,0:T(8,128)S(1)}, f32[2,88,128]{2,1,0:T(8,128)S(1)}, u32[]{:S(2)}, u32[]{:S(2)}) %collective-permute-start.46) | collective-permute-done | bytes 90144 | tf_op jit(solution)/shard_map/ppermute | solution.py:968
  450.0 4.2 collective-permute-done.47
  459.8 24.2 %all_to_all.97.refs_2_ = bf16[4,48,2304]{2,1,0:T(8,128)(2,1)S(1)} all-to-all(bf16[4,48,2304]{2,1,0:T(8,128)(2,1)} %shard_map.284), channel_id=1, replica_groups=mesh['doc'=4,'part'=4,'core'=2] {'doc'}, dimensions={0} | all-to-all | bytes 1769472 | tf_op jit(solution)/shard_map/all_to_all | solution.py:1000
  484.0 4.3 all-to-all-start.17
  491.8 26.8 %all-to-all-done.17.refs_1_ = bf16[4,48,3456]{2,1,0:T(8,128)(2,1)} async-done(((bf16[4,48,3456]{2,1,0:T(8,128)(2,1)}), bf16[4,48,3456]{2,1,0:T(8,128)(2,1)}, u32[]{:S(2)}, u32[]{:S(2)}) %all-to-all-start.17) | async-done | bytes 1327136 | tf_op jit(solution)/shard_map/all_to_all | solution.py:1000
  518.6 4.3 shard_map.285
  (224 shorter events, 126.4 us)
Async XLA Ops:
  0.7 53.0 %collective-permute-start.2 = (bf16[2,768,1536]{2,1,0:T(8,128)(2,1)}, bf16[2,768,1536]{2,1,0:T(8,128)(2,1)}, u32[]{:S(2)}, u32[]{:S(2)}) collective-permute-start(bf16[2,768,1536]{2,1,0:T(8,128)(2,1)} %refs_7_.7), channel_id=1, source_target_pairs={{0,1},{1,0},{2,3},{3,2},{4,5},{5,4},{6,7},{7,6},{8,9},{9,8},{10,11... | collective-permute-start | bytes 14155784 | tf_op jit(solution)/shard_map/ppermute | solution.py:968
  1.2 52.5 %collective-permute-start.3 = (bf16[2,1536,768]{2,1,0:T(8,128)(2,1)}, bf16[2,1536,768]{2,1,0:T(8,128)(2,1)}, u32[]{:S(2)}, u32[]{:S(2)}) collective-permute-start(bf16[2,1536,768]{2,1,0:T(8,128)(2,1)} %refs_6_.3), channel_id=1, source_target_pairs={{0,1},{1,0},{2,3},{3,2},{4,5},{5,4},{6,7},{7,6},{8,9},{9,8},{10,11... | collective-permute-start | bytes 14155784 | tf_op jit(solution)/shard_map/ppermute | solution.py:968
  6.7 46.9 %collective-permute-start = (bf16[2,768,1152]{2,1,0:T(8,128)(2,1)}, bf16[2,768,1152]{2,1,0:T(8,128)(2,1)}, u32[]{:S(2)}, u32[]{:S(2)}) collective-permute-start(bf16[2,768,1152]{2,1,0:T(8,128)(2,1)} %constant_dynamic-update-slice_fusion.refs_2_.refs_3_), channel_id=1, source_target_pairs={{0,1},{1,0},{2,3},{3,2},{4,5},{5,4},{6,7},{7,6},{8,9},{9,8},{10,11... | collective-permute-start | bytes 10616840 | tf_op jit(solution)/shard_map/ppermute | solution.py:968
  7.1 18.2 %all-to-all-start = ((bf16[4,64,768]{2,1,0:T(8,128)(2,1)}), bf16[4,64,768]{2,1,0:T(8,128)(2,1)S(1)}, u32[]{:S(2)}, u32[]{:S(2)}) async-start(bf16[4,64,768]{2,1,0:T(8,128)(2,1)} %param.15), calls=%async_computation | async-start | bytes 786432 | tf_op jit(solution)/shard_map/all_to_all | solution.py:1000
  25.8 17.7 %collective-permute-start.1 = (bf16[2,384,768]{2,1,0:T(8,128)(2,1)}, bf16[2,384,768]{2,1,0:T(8,128)(2,1)}, u32[]{:S(2)}, u32[]{:S(2)}) collective-permute-start(bf16[2,384,768]{2,1,0:T(8,128)(2,1)} %refs_10_.7), channel_id=1, source_target_pairs={{0,1},{1,0},{2,3},{3,2},{4,5},{5,4},{6,7},{7,6},{8,9},{9,8},{10,11... | collective-permute-start | bytes 3538952 | tf_op jit(solution)/shard_map/ppermute | solution.py:968
  27.0 15.7 %collective-permute-start.6 = (f32[2,6,33]{2,1,0:T(8,128)S(1)}, f32[2,6,33]{2,1,0:T(8,128)S(1)}, u32[]{:S(2)}, u32[]{:S(2)}) collective-permute-start(f32[2,6,33]{2,1,0:T(8,128)S(1)} %copy.42), channel_id=1, source_target_pairs={{0,1},{1,0},{2,3},{3,2},{4,5},{5,4},{6,7},{7,6},{8,9},{9,8},{10,11... | collective-permute-start | bytes 4760 | tf_op jit(solution)/shard_map/ppermute | solution.py:968
  28.0 10.9 %all-to-all-start.2 = ((f32[4,64,384]{2,1,0:T(8,128)}), f32[4,64,384]{2,1,0:T(8,128)S(1)}, u32[]{:S(2)}, u32[]{:S(2)}) async-start(f32[4,64,384]{2,1,0:T(8,128)} %broadcast_in_dim.8), calls=%async_computation.2 | async-start | bytes 786432 | tf_op jit(solution)/shard_map/all_to_all | solution.py:1000
  38.8 14.8 %all-to-all-start.1 = ((bf16[4,64,768]{2,1,0:T(8,128)(2,1)}), bf16[4,64,768]{2,1,0:T(8,128)(2,1)S(1)}, u32[]{:S(2)}, u32[]{:S(2)}) async-start(bf16[4,64,768]{2,1,0:T(8,128)(2,1)} %param.16), calls=%async_computation.1 | async-start | bytes 786432 | tf_op jit(solution)/shard_map/all_to_all | solution.py:1000
  42.8 15.8 %collective-permute-start.8 = (f32[64,384]{1,0:T(8,128)S(1)}, f32[64,384]{1,0:T(8,128)S(1)}, u32[]{:S(2)}, u32[]{:S(2)}) collective-permute-start(f32[64,384]{1,0:T(8,128)S(1)} %fusion.5.refs_0_), channel_id=1, source_target_pairs={{0,1},{1,0},{2,3},{3,2},{4,5},{5,4},{6,7},{7,6},{8,9},{9,8},{10,11... | collective-permute-start | bytes 294920 | tf_op jit(solution)/shard_map/ppermute | solution.py:968
  43.5 26.9 %collective-permute-start.9 = (f32[2,1536]{1,0:T(2,128)S(1)}, f32[2,1536]{1,0:T(2,128)S(1)}, u32[]{:S(2)}, u32[]{:S(2)}) collective-permute-start(f32[2,1536]{1,0:T(2,128)S(1)} %copy-done.26), channel_id=1, source_target_pairs={{0,1},{1,0},{2,3},{3,2},{4,5},{5,4},{6,7},{7,6},{8,9},{9,8},{10,11... | collective-permute-start | bytes 36872 | tf_op jit(solution)/shard_map/ppermute | solution.py:968
  66.9 13.6 %all-to-all-start.3 = ((f32[8,72,128]{2,1,0:T(8,128)}), f32[8,72,128]{2,1,0:T(8,128)S(1)}, u32[]{:S(2)}, u32[]{:S(2)}) async-start(f32[8,72,128]{2,1,0:T(8,128)} %get-tuple-element.124), calls=%async_computation.3 | async-start | bytes 589824 | tf_op jit(solution)/shard_map/all_to_all | solution.py:1000
  70.4 15.2 %collective-permute-start.4 = (f32[64,768]{1,0:T(8,128)S(1)}, f32[64,768]{1,0:T(8,128)S(1)}, u32[]{:S(2)}, u32[]{:S(2)}) collective-permute-start(f32[64,768]{1,0:T(8,128)S(1)} %get-tuple-element.122), channel_id=1, source_target_pairs={{0,1},{1,2},{2,3},{3,4},{4,5},{5,6},{6,7},{7,0},{8,9},{9,10},{10,1... | collective-permute-start | bytes 589832 | tf_op jit(solution)/shard_map/ppermute | solution.py:1007
  70.8 14.8 %collective-permute-start.5 = (f32[64,768]{1,0:T(8,128)S(1)}, f32[64,768]{1,0:T(8,128)S(1)}, u32[]{:S(2)}, u32[]{:S(2)}) collective-permute-start(f32[64,768]{1,0:T(8,128)S(1)} %get-tuple-element.123), channel_id=1, source_target_pairs={{1,0},{2,1},{3,2},{4,3},{5,4},{6,5},{7,6},{0,7},{9,8},{10,9},{11,1... | collective-permute-start | bytes 589832 | tf_op jit(solution)/shard_map/ppermute | solution.py:1008
  82.0 10.9 %all-to-all-start.4 = ((f32[8,72,128]{2,1,0:T(8,128)}), f32[8,72,128]{2,1,0:T(8,128)S(1)}, u32[]{:S(2)}, u32[]{:S(2)}) async-start(f32[8,72,128]{2,1,0:T(8,128)} %get-tuple-element.127), calls=%async_computation.4 | async-start | bytes 589824 | tf_op jit(solution)/shard_map/all_to_all | solution.py:1000
  146.8 15.2 %all-to-all-start.7 = ((f32[8,72,128]{2,1,0:T(8,128)}), f32[8,72,128]{2,1,0:T(8,128)S(1)}, u32[]{:S(2)}, u32[]{:S(2)}) async-start(f32[8,72,128]{2,1,0:T(8,128)} %get-tuple-element.138), calls=%async_computation.7 | async-start | bytes 589824 | tf_op jit(solution)/shard_map/all_to_all | solution.py:1000
  151.0 11.0 %collective-permute-start.10 = (f32[64,768]{1,0:T(8,128)}, f32[64,768]{1,0:T(8,128)S(1)}, u32[]{:S(2)}, u32[]{:S(2)}) collective-permute-start(f32[64,768]{1,0:T(8,128)} %copy-done.20), channel_id=1, source_target_pairs={{0,1},{1,2},{2,3},{3,4},{4,5},{5,6},{6,7},{7,0},{8,9},{9,10},{10,1... | collective-permute-start | bytes 589832 | tf_op jit(solution)/shard_map/ppermute | solution.py:1007
  192.0 17.5 %all-to-all-start.9 = ((f32[8,128,128]{2,1,0:T(8,128)}), f32[8,128,128]{2,1,0:T(8,128)}, u32[]{:S(2)}, u32[]{:S(2)}) async-start(f32[8,128,128]{2,1,0:T(8,128)} %get-tuple-element.148), calls=%async_computation.9 | async-start | bytes 1048576 | tf_op jit(solution)/shard_map/all_to_all | solution.py:1000
  196.2 13.4 %collective-permute-start.14 = (f32[64,768]{1,0:T(8,128)}, f32[64,768]{1,0:T(8,128)S(1)}, u32[]{:S(2)}, u32[]{:S(2)}) collective-permute-start(f32[64,768]{1,0:T(8,128)} %copy-done.21), channel_id=1, source_target_pairs={{0,1},{1,2},{2,3},{3,4},{4,5},{5,6},{6,7},{7,0},{8,9},{9,10},{10,1... | collective-permute-start | bytes 589832 | tf_op jit(solution)/shard_map/ppermute | solution.py:1007
  196.6 13.0 %collective-permute-start.15 = (f32[64,768]{1,0:T(8,128)S(1)}, f32[64,768]{1,0:T(8,128)S(1)}, u32[]{:S(2)}, u32[]{:S(2)}) collective-permute-start(f32[64,768]{1,0:T(8,128)S(1)} %get-tuple-element.151), channel_id=1, source_target_pairs={{1,0},{2,1},{3,2},{4,3},{5,4},{6,5},{7,6},{0,7},{9,8},{10,9},{11,1... | collective-permute-start | bytes 589832 | tf_op jit(solution)/shard_map/ppermute | solution.py:1008
  199.1 59.9 %collective-permute-start.19 = (bf16[256,3456]{1,0:T(8,128)(2,1)}, bf16[256,3456]{1,0:T(8,128)(2,1)}, u32[]{:S(2)}, u32[]{:S(2)}) collective-permute-start(bf16[256,3456]{1,0:T(8,128)(2,1)} %get-tuple-element.162.refs_3_), channel_id=1, source_target_pairs={{0,1},{1,0},{2,3},{3,2},{4,5},{5,4},{6,7},{7,6},{8,9},{9,8},{10,11... | collective-permute-start | bytes 5308424 | tf_op jit(solution)/shard_map/ppermute | solution.py:968
  219.5 17.2 %all-to-all-start.10 = ((f32[8,200,128]{2,1,0:T(8,128)}), f32[8,200,128]{2,1,0:T(8,128)}, u32[]{:S(2)}, u32[]{:S(2)}) async-start(f32[8,200,128]{2,1,0:T(8,128)} %shard_map.266.refs_7_), calls=%async_computation.10 | async-start | bytes 1638400 | tf_op jit(solution)/shard_map/all_to_all | solution.py:1000
  223.8 35.2 %collective-permute-start.18 = (bf16[256,3072]{1,0:T(8,128)(2,1)}, bf16[256,3072]{1,0:T(8,128)(2,1)}, u32[]{:S(2)}, u32[]{:S(2)}) collective-permute-start(bf16[256,3072]{1,0:T(8,128)(2,1)} %get-tuple-element.160.refs_0_), channel_id=1, source_target_pairs={{0,1},{1,0},{2,3},{3,2},{4,5},{5,4},{6,7},{7,6},{8,9},{9,8},{10,11... | collective-permute-start | bytes 4718600 | tf_op jit(solution)/shard_map/ppermute | solution.py:968
  254.4 26.5 %all-to-all-start.8 = ((f32[4,64,768]{2,1,0:T(8,128)}), f32[4,64,768]{2,1,0:T(8,128)}, u32[]{:S(2)}, u32[]{:S(2)}) async-start(f32[4,64,768]{2,1,0:T(8,128)} %bitcast.46), calls=%async_computation.8 | async-start | bytes 1572864 | tf_op jit(solution)/shard_map/all_to_all | solution.py:1000
  271.2 35.6 %collective-permute-start.22 = (bf16[384,1920]{1,0:T(8,128)(2,1)}, bf16[384,1920]{1,0:T(8,128)(2,1)}, u32[]{:S(2)}, u32[]{:S(2)}) collective-permute-start(bf16[384,1920]{1,0:T(8,128)(2,1)} %get-tuple-element.176), channel_id=1, source_target_pairs={{0,2},{2,0},{4,6},{6,4},{1,3},{3,1},{5,7},{7,5},{8,10},{10,8},{12,... | collective-permute-start | bytes 4423688 | tf_op jit(solution)/shard_map/ppermute | solution.py:968
  272.2 29.1 %collective-permute-start.23 = (bf16[384,1536]{1,0:T(8,128)(2,1)}, bf16[384,1536]{1,0:T(8,128)(2,1)}, u32[]{:S(2)}, u32[]{:S(2)}) collective-permute-start(bf16[384,1536]{1,0:T(8,128)(2,1)} %get-tuple-element.178), channel_id=1, source_target_pairs={{0,4},{2,6},{4,0},{6,2},{1,5},{3,7},{5,1},{7,3},{8,12},{10,14},{12... | collective-permute-start | bytes 3538952 | tf_op jit(solution)/shard_map/ppermute | solution.py:968
  294.7 18.8 %all-to-all-start.12 = ((f32[8,128,128]{2,1,0:T(8,128)}), f32[8,128,128]{2,1,0:T(8,128)S(1)}, u32[]{:S(2)}, u32[]{:S(2)}) async-start(f32[8,128,128]{2,1,0:T(8,128)} %get-tuple-element.172), calls=%async_computation.12 | async-start | bytes 1048576 | tf_op jit(solution)/shard_map/all_to_all | solution.py:1000
  298.2 55.1 %collective-permute-start.29 = (bf16[256,3456]{1,0:T(8,128)(2,1)}, bf16[256,3456]{1,0:T(8,128)(2,1)}, u32[]{:S(2)}, u32[]{:S(2)}) collective-permute-start(bf16[256,3456]{1,0:T(8,128)(2,1)} %get-tuple-element.194.refs_3_.refs_4_), channel_id=1, source_target_pairs={{0,1},{1,0},{2,3},{3,2},{4,5},{5,4},{6,7},{7,6},{8,9},{9,8},{10,11... | collective-permute-start | bytes 5308424 | tf_op jit(solution)/shard_map/ppermute | solution.py:968
  298.6 14.9 %collective-permute-start.20 = (f32[64,768]{1,0:T(8,128)}, f32[64,768]{1,0:T(8,128)S(1)}, u32[]{:S(2)}, u32[]{:S(2)}) collective-permute-start(f32[64,768]{1,0:T(8,128)} %get-tuple-element.174), channel_id=1, source_target_pairs={{0,1},{1,2},{2,3},{3,4},{4,5},{5,6},{6,7},{7,0},{8,9},{9,10},{10,1... | collective-permute-start | bytes 589832 | tf_op jit(solution)/shard_map/ppermute | solution.py:1007
  298.8 14.7 %collective-permute-start.21 = (f32[64,768]{1,0:T(8,128)S(1)}, f32[64,768]{1,0:T(8,128)S(1)}, u32[]{:S(2)}, u32[]{:S(2)}) collective-permute-start(f32[64,768]{1,0:T(8,128)S(1)} %get-tuple-element.175), channel_id=1, source_target_pairs={{1,0},{2,1},{3,2},{4,3},{5,4},{6,5},{7,6},{0,7},{9,8},{10,9},{11,1... | collective-permute-start | bytes 589832 | tf_op jit(solution)/shard_map/ppermute | solution.py:1008
  301.2 52.1 %collective-permute-start.28 = (bf16[256,3072]{1,0:T(8,128)(2,1)}, bf16[256,3072]{1,0:T(8,128)(2,1)}, u32[]{:S(2)}, u32[]{:S(2)}) collective-permute-start(bf16[256,3072]{1,0:T(8,128)(2,1)} %get-tuple-element.192.refs_0_), channel_id=1, source_target_pairs={{0,1},{1,0},{2,3},{3,2},{4,5},{5,4},{6,7},{7,6},{8,9},{9,8},{10,11... | collective-permute-start | bytes 4718600 | tf_op jit(solution)/shard_map/ppermute | solution.py:968
  322.3 18.1 %all-to-all-start.13 = ((f32[8,200,128]{2,1,0:T(8,128)}), f32[8,200,128]{2,1,0:T(8,128)}, u32[]{:S(2)}, u32[]{:S(2)}) async-start(f32[8,200,128]{2,1,0:T(8,128)} %shard_map.273.refs_7_), calls=%async_computation.13 | async-start | bytes 1638400 | tf_op jit(solution)/shard_map/all_to_all | solution.py:1000
  327.0 38.5 %collective-permute-start.26 = (bf16[192,1920]{1,0:T(8,128)(2,1)}, bf16[192,1920]{1,0:T(8,128)(2,1)}, u32[]{:S(2)}, u32[]{:S(2)}) collective-permute-start(bf16[192,1920]{1,0:T(8,128)(2,1)} %get-tuple-element.189), channel_id=1, source_target_pairs={{0,4},{2,6},{4,0},{6,2},{1,5},{3,7},{5,1},{7,3},{8,12},{10,14},{12... | collective-permute-start | bytes 2211848 | tf_op jit(solution)/shard_map/ppermute | solution.py:968
  329.0 36.5 %collective-permute-start.27 = (bf16[192,1536]{1,0:T(8,128)(2,1)S(1)}, bf16[192,1536]{1,0:T(8,128)(2,1)}, u32[]{:S(2)}, u32[]{:S(2)}) collective-permute-start(bf16[192,1536]{1,0:T(8,128)(2,1)S(1)} %copy-done.17), channel_id=1, source_target_pairs={{0,2},{2,0},{4,6},{6,4},{1,3},{3,1},{5,7},{7,5},{8,10},{10,8},{12,... | collective-permute-start | bytes 1769480 | tf_op jit(solution)/shard_map/ppermute | solution.py:968
  348.7 20.1 %all-to-all-start.14 = ((f32[4,64,384]{2,1,0:T(8,128)}), f32[4,64,384]{2,1,0:T(8,128)}, u32[]{:S(2)}, u32[]{:S(2)}) async-start(f32[4,64,384]{2,1,0:T(8,128)} %broadcast_in_dim.11), calls=%async_computation.14 | async-start | bytes 786432 | tf_op jit(solution)/shard_map/all_to_all | solution.py:1000
  368.8 36.8 %all-to-all-start.16 = ((bf16[4,48,3456]{2,1,0:T(8,128)(2,1)}), bf16[4,48,3456]{2,1,0:T(8,128)(2,1)}, u32[]{:S(2)}, u32[]{:S(2)}) async-start(bf16[4,48,3456]{2,1,0:T(8,128)(2,1)} %shard_map.277.refs_11_), calls=%async_computation.16 | async-start | bytes 2654208 | tf_op jit(solution)/shard_map/all_to_all | solution.py:1000
  373.5 35.8 %collective-permute-start.30 = (bf16[384,1920]{1,0:T(8,128)(2,1)}, bf16[384,1920]{1,0:T(8,128)(2,1)}, u32[]{:S(2)}, u32[]{:S(2)}) collective-permute-start(bf16[384,1920]{1,0:T(8,128)(2,1)} %get-tuple-element.198), channel_id=1, source_target_pairs={{0,2},{2,0},{4,6},{6,4},{1,3},{3,1},{5,7},{7,5},{8,10},{10,8},{12,... | collective-permute-start | bytes 4423688 | tf_op jit(solution)/shard_map/ppermute | solution.py:968
  377.1 32.1 %collective-permute-start.31 = (bf16[384,1536]{1,0:T(8,128)(2,1)}, bf16[384,1536]{1,0:T(8,128)(2,1)}, u32[]{:S(2)}, u32[]{:S(2)}) collective-permute-start(bf16[384,1536]{1,0:T(8,128)(2,1)} %get-tuple-element.200), channel_id=1, source_target_pairs={{0,4},{2,6},{4,0},{6,2},{1,5},{3,7},{5,1},{7,3},{8,12},{10,14},{12... | collective-permute-start | bytes 3538952 | tf_op jit(solution)/shard_map/ppermute | solution.py:968
  395.9 38.8 %collective-permute-start.37 = (bf16[384,1152]{1,0:T(8,128)(2,1)}, bf16[384,1152]{1,0:T(8,128)(2,1)}, u32[]{:S(2)}, u32[]{:S(2)}) collective-permute-start(bf16[384,1152]{1,0:T(8,128)(2,1)} %get-tuple-element.210), channel_id=1, source_target_pairs={{0,2},{2,0},{4,6},{6,4},{1,3},{3,1},{5,7},{7,5},{8,10},{10,8},{12,... | collective-permute-start | bytes 2654216 | tf_op jit(solution)/shard_map/ppermute | solution.py:968
  396.5 38.2 %collective-permute-start.38 = (bf16[384,1152]{1,0:T(8,128)(2,1)}, bf16[384,1152]{1,0:T(8,128)(2,1)}, u32[]{:S(2)}, u32[]{:S(2)}) collective-permute-start(bf16[384,1152]{1,0:T(8,128)(2,1)} %get-tuple-element.212), channel_id=1, source_target_pairs={{0,4},{2,6},{4,0},{6,2},{1,5},{3,7},{5,1},{7,3},{8,12},{10,14},{12... | collective-permute-start | bytes 2654216 | tf_op jit(solution)/shard_map/ppermute | solution.py:968
  405.6 29.1 %all-to-all-start.15 = ((bf16[4,64,768]{2,1,0:T(8,128)(2,1)}), bf16[4,64,768]{2,1,0:T(8,128)(2,1)S(1)}, u32[]{:S(2)}, u32[]{:S(2)}) async-start(bf16[4,64,768]{2,1,0:T(8,128)(2,1)} %bitcast.9), calls=%async_computation.15 | async-start | bytes 786432 | tf_op jit(solution)/shard_map/all_to_all | solution.py:1000
  416.1 13.6 %collective-permute-start.40 = (f32[2,88,128]{2,1,0:T(8,128)S(1)}, f32[2,88,128]{2,1,0:T(8,128)S(1)}, u32[]{:S(2)}, u32[]{:S(2)}) collective-permute-start(f32[2,88,128]{2,1,0:T(8,128)S(1)} %add.168), channel_id=1, source_target_pairs={{0,2},{2,0},{4,6},{6,4},{1,3},{3,1},{5,7},{7,5},{8,10},{10,8},{12,... | collective-permute-start | bytes 270344 | tf_op jit(solution)/shard_map/ppermute | solution.py:968
  417.9 13.6 %collective-permute-start.41 = (f32[2,88,128]{2,1,0:T(8,128)S(1)}, f32[2,88,128]{2,1,0:T(8,128)S(1)}, u32[]{:S(2)}, u32[]{:S(2)}) collective-permute-start(f32[2,88,128]{2,1,0:T(8,128)S(1)} %add.168), channel_id=1, source_target_pairs={{0,4},{2,6},{4,0},{6,2},{1,5},{3,7},{5,1},{7,3},{8,12},{10,14},{12... | collective-permute-start | bytes 270344 | tf_op jit(solution)/shard_map/ppermute | solution.py:968
  419.3 13.6 %collective-permute-start.42 = (f32[2,88,128]{2,1,0:T(8,128)S(1)}, f32[2,88,128]{2,1,0:T(8,128)S(1)}, u32[]{:S(2)}, u32[]{:S(2)}) collective-permute-start(f32[2,88,128]{2,1,0:T(8,128)S(1)} %add.168), channel_id=1, source_target_pairs={{0,6},{2,4},{4,2},{6,0},{1,7},{3,5},{5,3},{7,1},{8,14},{10,12},{12... | collective-permute-start | bytes 270344 | tf_op jit(solution)/shard_map/ppermute | solution.py:968
  429.7 24.5 %collective-permute-start.35 = (bf16[192,1920]{1,0:T(8,128)(2,1)}, bf16[192,1920]{1,0:T(8,128)(2,1)}, u32[]{:S(2)}, u32[]{:S(2)}) collective-permute-start(bf16[192,1920]{1,0:T(8,128)(2,1)} %get-tuple-element.207), channel_id=1, source_target_pairs={{0,4},{2,6},{4,0},{6,2},{1,5},{3,7},{5,1},{7,3},{8,12},{10,14},{12... | collective-permute-start | bytes 2211848 | tf_op jit(solution)/shard_map/ppermute | solution.py:968
  431.4 22.8 %collective-permute-start.36 = (bf16[192,1536]{1,0:T(8,128)(2,1)}, bf16[192,1536]{1,0:T(8,128)(2,1)S(1)}, u32[]{:S(2)}, u32[]{:S(2)}) collective-permute-start(bf16[192,1536]{1,0:T(8,128)(2,1)} %get-tuple-element.209), channel_id=1, source_target_pairs={{0,2},{2,0},{4,6},{6,4},{1,3},{3,1},{5,7},{7,5},{8,10},{10,8},{12,... | collective-permute-start | bytes 1769480 | tf_op jit(solution)/shard_map/ppermute | solution.py:968
  438.7 18.6 %collective-permute-start.43 = (bf16[192,1152]{1,0:T(8,128)(2,1)S(1)}, bf16[192,1152]{1,0:T(8,128)(2,1)S(1)}, u32[]{:S(2)}, u32[]{:S(2)}) collective-permute-start(bf16[192,1152]{1,0:T(8,128)(2,1)S(1)} %get-tuple-element.219), channel_id=1, source_target_pairs={{0,4},{2,6},{4,0},{6,2},{1,5},{3,7},{5,1},{7,3},{8,12},{10,14},{12... | collective-permute-start | bytes 1327112 | tf_op jit(solution)/shard_map/ppermute | solution.py:968
  439.3 18.0 %collective-permute-start.44 = (bf16[192,1152]{1,0:T(8,128)(2,1)}, bf16[192,1152]{1,0:T(8,128)(2,1)S(1)}, u32[]{:S(2)}, u32[]{:S(2)}) collective-permute-start(bf16[192,1152]{1,0:T(8,128)(2,1)} %get-tuple-element.221), channel_id=1, source_target_pairs={{0,2},{2,0},{4,6},{6,4},{1,3},{3,1},{5,7},{7,5},{8,10},{10,8},{12,... | collective-permute-start | bytes 1327112 | tf_op jit(solution)/shard_map/ppermute | solution.py:968
  484.0 34.6 %all-to-all-start.17 = ((bf16[4,48,3456]{2,1,0:T(8,128)(2,1)}), bf16[4,48,3456]{2,1,0:T(8,128)(2,1)}, u32[]{:S(2)}, u32[]{:S(2)}) async-start(bf16[4,48,3456]{2,1,0:T(8,128)(2,1)} %shard_map.283.refs_4_), calls=%async_computation.17 | async-start | bytes 2654208 | tf_op jit(solution)/shard_map/all_to_all | solution.py:1000
  (47 other events, 579.3 us)
